TPU v7x, 1024 devices: a whole 4x4x32 slice. The times are simulated.
1024 devices in a mesh: dom: 256 (over x, z, core), grp: 4 (over y).
Axes of the slice: x: 4, y: 4, z: 32, core: 2. Of those that a mesh axis runs over, the one named last changes fastest.
Arguments:
- residual: float32 [256, 4, 12, 4096], P('dom', None, 'grp'), may hold values from -6 to 6
- orders: int32 [256, 4, 12], P('dom', None, 'grp'), may hold values from 7 to 15
- factors: float32 [256, 4, 12, 4], P('dom', None, 'grp'), may hold values from 0.3 to 3
- widths: int32 [4], replicated, may hold values from 1 to 3, 8 in all
Outputs:
- correction: float32 [256, 4, 12, 4096], P('dom', None, 'grp')
Inputs may be any that keep to these rules, and one draw needn't show every extreme that they name: Each strip is 1 to 3 layers wide, the widths sum to 8, and at least one strip, and at most two, is exactly 3 wide.
All inputs are finite; a program needn't handle non-finite values.
Results may differ from a plain program's by a relative error of at most 0.0003.
Values sent between devices are 32-bit elements; how exact they have to be, the bound alone decides.
A program may use at most 64 MiB of HBM per device.

v0:
```python
import functools

import jax
import jax.numpy as jnp
import numpy as np
from jax import lax
from jax.sharding import PartitionSpec as P

precise = lax.Precision.HIGHEST
mass_weight = 0.5
penalty = 0.5
cheb_high = 4.0
cheb_low = 0.15


def with_halo(block, sides, width):
    for axis, dim in sides:
        count = lax.axis_size(axis)
        forward = [(i, i + 1) for i in range(count - 1)]
        forward.append((count - 1, 0))
        backward = [(target, source) for source, target in forward]
        low = lax.ppermute(
            lax.slice_in_dim(block, block.shape[dim] - width, None, axis=dim), axis, forward
        )
        high = lax.ppermute(lax.slice_in_dim(block, 0, width, axis=dim), axis, backward)
        block = jnp.concatenate([low, block, high], axis=dim)
    return block


def cheb_nodes(degree):
    return -np.cos(np.pi * np.arange(degree + 1) / degree)


def bary_weights(npoints):
    weights = (-1.0) ** np.arange(npoints)
    weights[0] = 0.5 * weights[0]
    weights[-1] = 0.5 * weights[-1]
    return weights


def lagrange_table(source, target):
    weights = bary_weights(source.shape[0])
    spacing = target[:, None] - source[None, :]
    coincide = np.abs(spacing) < 1e-12
    fractions = weights[None, :] / np.where(coincide, 1.0, spacing)
    lookup = fractions / fractions.sum(axis=1, keepdims=True)
    return np.where(coincide.any(axis=1, keepdims=True), np.where(coincide, 1.0, 0.0), lookup)


def quad_weights(degree):
    weights = np.full(degree + 1, np.pi / degree)
    weights[0] = 0.5 * weights[0]
    weights[-1] = 0.5 * weights[-1]
    return weights


def derivative(degree):
    points = cheb_nodes(degree)
    weights = bary_weights(degree + 1)
    spacing = points[:, None] - points[None, :] + np.eye(degree + 1)
    lookup = weights[None, :] / weights[:, None] / spacing
    lookup = lookup * (1.0 - np.eye(degree + 1))
    return lookup - np.eye(degree + 1) * lookup.sum(axis=1)[:, None]


def level_degree(degree, level_index):
    return [degree, degree // 2, 1][level_index]


def level_tables(level_index):
    points = [16, 8, 2][level_index]
    common = cheb_nodes(points - 1)
    common_w = quad_weights(points - 1)
    stiffness, quad_w, last_pick, interpolate, face_diag, living, prolong_pick = (
        [],
        [],
        [],
        [],
        [],
        [],
        [],
    )
    for degree in range(7, 16):
        local = level_degree(degree, level_index)
        deriv_mat = derivative(local)
        quad_wts = quad_weights(local)
        stiff_pad = np.zeros((points, points))
        stiff_pad[: local + 1, : local + 1] = deriv_mat.T @ (quad_wts[:, None] * deriv_mat)
        quad_pad = np.zeros(points)
        quad_pad[: local + 1] = quad_wts
        last_vec = np.zeros(points)
        last_vec[local] = 1.0
        interp_pad = np.zeros((points, points))
        interp_pad[:, : local + 1] = lagrange_table(cheb_nodes(local), common)
        stiffness.append(stiff_pad)
        quad_w.append(quad_pad)
        last_pick.append(last_vec)
        interpolate.append(interp_pad)
        face_diag.append((common_w[:, None] * interp_pad**2).sum(axis=0))
        living.append(np.where(np.arange(points) <= local, 1.0, 0.0))
        if level_index < 2:
            next_points = [16, 8, 2][level_index + 1]
            coarse = level_degree(degree, level_index + 1)
            prolong_pad = np.zeros((points, next_points))
            prolong_pad[: local + 1, : coarse + 1] = lagrange_table(
                cheb_nodes(coarse), cheb_nodes(local)
            )
            prolong_pick.append(prolong_pad)
    lookup = {
        "stiffness": stiffness,
        "quad_w": quad_w,
        "last_pick": last_pick,
        "interpolate": interpolate,
        "face_diag": face_diag,
        "living": living,
    }
    if level_index < 2:
        lookup["prolong_pick"] = prolong_pick
    lookup = {entry: np.stack(lookup[entry]).astype(np.float32) for entry in lookup}
    factor_tau = penalty * (points - 1) ** 2
    lookup["tau"] = factor_tau
    lookup["pair"] = (factor_tau * np.outer(common_w, common_w)).astype(np.float32)
    first_vec = np.zeros(points)
    first_vec[0] = 1.0
    lookup["first_pick"] = first_vec.astype(np.float32)
    lookup["points"] = points
    return lookup


def lane_rows(table, points):
    return jnp.repeat(jnp.transpose(table), points, axis=1)


def block_size(elements):
    for candidate in range(elements, 0, -1):
        return candidate
    return 1


def block_diag(mats, per_block):
    elements, rows_a, cols_b = mats.shape
    groups = elements // per_block
    grouped = mats.reshape(groups, per_block, rows_a, cols_b)
    identity = jnp.eye(per_block, dtype=jnp.float32)
    full = identity[None, :, None, :, None] * grouped[:, :, :, None, :]
    return full.reshape(groups, per_block * rows_a, per_block * cols_b)


def setup_level(lookup, onehot, factors, element_mask):

    def select_rows(entry):
        return jnp.einsum("ec,c...->e...", onehot, jnp.asarray(lookup[entry]), precision=precise)

    points = lookup["points"]
    elements = onehot.shape[0]
    per_block = block_size(elements)
    stiffness = select_rows("stiffness")
    quad_w = select_rows("quad_w")
    last_pick = select_rows("last_pick")
    face_diag = select_rows("face_diag")
    living = select_rows("living")
    first_pick = jnp.asarray(lookup["first_pick"])
    setup = {
        "points": points,
        "interpolate": select_rows("interpolate"),
        "pair": jnp.asarray(lookup["pair"]),
        "first_pick": first_pick,
    }
    weight_rows = lane_rows(quad_w, points)
    weight_lanes = quad_w.reshape(-1)
    stiff_diag = jnp.diagonal(stiffness, axis1=1, axis2=2)
    diag_rows = lane_rows(stiff_diag, points)
    diag_lanes = stiff_diag.reshape(-1)
    ends = first_pick[None, :] + last_pick
    ends_rows = lane_rows(ends, points)
    ends_lanes = ends.reshape(-1)
    face_rows = lane_rows(face_diag, points)
    face_lanes = face_diag.reshape(-1)
    live_rows = lane_rows(living, points)
    live_lanes = living.reshape(-1)
    mask_lanes = jnp.repeat(element_mask, points)
    factor_lanes = [jnp.repeat(factors[:, column], points) for column in range(4)]
    weight_i = weight_rows[:, None, :]
    weight_j = weight_rows[None, :, :]
    diagonal = (
        factor_lanes[0] * diag_rows[:, None, :] * weight_j * weight_lanes
        + factor_lanes[1] * weight_i * diag_rows[None, :, :] * weight_lanes
        + factor_lanes[2] * weight_i * weight_j * diag_lanes
        + factor_lanes[3] * mass_weight * weight_i * weight_j * weight_lanes
        + lookup["tau"]
        * (
            ends_rows[:, None, :] * face_rows[None, :, :] * face_lanes
            + face_rows[:, None, :] * ends_rows[None, :, :] * face_lanes
            + face_rows[:, None, :] * face_rows[None, :, :] * ends_lanes
        )
    )
    node_live = live_rows[:, None, :] * live_rows[None, :, :] * live_lanes * mask_lanes
    setup["node_live"] = node_live
    setup["mask_lanes"] = mask_lanes
    setup["dinv"] = node_live / (diagonal + 1.0 - node_live)
    setup["stiff_lanes"] = jnp.repeat(jnp.transpose(stiffness, (1, 2, 0)), points, axis=2)
    setup["stiff_blocks"] = block_diag(stiffness, per_block)
    setup["coeff_x"] = factor_lanes[0] * weight_j * weight_lanes
    setup["coeff_y"] = factor_lanes[1] * weight_i * weight_lanes
    setup["coeff_z"] = factor_lanes[2] * weight_i * weight_j
    setup["coeff_m"] = factor_lanes[3] * mass_weight * weight_i * weight_j * weight_lanes
    setup["last_lanes"] = lane_rows(last_pick, points)
    identity = jnp.eye(elements, dtype=jnp.float32)
    first_part = (identity[:, None, :] * first_pick[None, :, None]).reshape(
        elements * points, elements
    )
    last_part = (identity[:, None, :] * last_pick[:, :, None]).reshape(elements * points, elements)
    setup["face_pick"] = jnp.concatenate([first_part, last_part], axis=1)
    if "prolong_pick" in lookup:
        prolong_pick = select_rows("prolong_pick")
        setup["prolong_lanes"] = jnp.repeat(jnp.transpose(prolong_pick, (1, 2, 0)), points, axis=2)
        setup["prolong_blocks"] = block_diag(prolong_pick, per_block)
    return setup


def build_levels(orders_flat, factors_flat, element_mask):
    onehot = (orders_flat[:, None] == jnp.arange(7, 16)[None, :]).astype(jnp.float32)
    return [
        setup_level(level_tables(level_index), onehot, factors_flat, element_mask)
        for level_index in range(3)
    ]


def volume(values, setup):
    points = setup["points"]
    stiff_lanes = setup["stiff_lanes"]
    along_x = jnp.sum(stiff_lanes[:, :, None, :] * values[None], axis=1)
    along_y = jnp.sum(stiff_lanes[None] * values[:, None], axis=2)
    blocks = setup["stiff_blocks"]
    grouped = values.reshape(points, points, blocks.shape[0], -1)
    along_z = jnp.einsum("ijgb,gab->ijga", grouped, blocks, precision=precise).reshape(
        points, points, -1
    )
    return (
        setup["coeff_x"] * along_x
        + setup["coeff_y"] * along_y
        + setup["coeff_z"] * along_z
        + setup["coeff_m"] * values
    )


def traces(values, setup):
    points = setup["points"]
    elements = values.shape[2] // points
    last_lanes = setup["last_lanes"]
    interpolate = setup["interpolate"]

    def to_elements(face):
        return jnp.transpose(face.reshape(face.shape[0], elements, points), (1, 0, 2))

    k_faces = jnp.einsum("ijq,qf->ijf", values, setup["face_pick"], precision=precise)
    raw_faces = [
        to_elements(values[0]),
        to_elements(jnp.sum(values * last_lanes[:, None, :], axis=0)),
        to_elements(values[:, 0]),
        to_elements(jnp.sum(values * last_lanes[None, :, :], axis=1)),
        jnp.transpose(k_faces[:, :, :elements], (2, 0, 1)),
        jnp.transpose(k_faces[:, :, elements:], (2, 0, 1)),
    ]
    common_faces = []
    for face in raw_faces:
        halfway = jnp.einsum("ebj,ejk->ebk", interpolate, face, precision=precise)
        common_faces.append(jnp.einsum("eck,ebk->ebc", interpolate, halfway, precision=precise))
    return common_faces


def face_apply(setup, own_traces, nearby):
    interpolate = setup["interpolate"]
    returned = []
    for own_trace, near_trace in zip(own_traces, nearby):
        jump_term = setup["pair"][None] * (own_trace - near_trace)
        halfway = jnp.einsum("ebc,eck->ebk", jump_term, interpolate, precision=precise)
        returned.append(jnp.einsum("ebj,ebk->ejk", interpolate, halfway, precision=precise))

    def to_lanes(array):
        return jnp.transpose(array, (1, 0, 2)).reshape(array.shape[1], -1)

    first_pick = setup["first_pick"]
    last_lanes = setup["last_lanes"]
    total = (
        first_pick[:, None, None] * to_lanes(returned[0])[None]
        + last_lanes[:, None, :] * to_lanes(returned[1])[None]
        + first_pick[None, :, None] * to_lanes(returned[2])[:, None, :]
        + last_lanes[None, :, :] * to_lanes(returned[3])[:, None, :]
    )
    k_part = jnp.concatenate(
        [jnp.transpose(returned[4], (1, 2, 0)), jnp.transpose(returned[5], (1, 2, 0))], axis=2
    )
    return total + jnp.einsum("ijf,qf->ijq", k_part, setup["face_pick"], precision=precise)


def smooth(rhs, setup, operate):
    centre = 0.5 * (cheb_high + cheb_low)
    radius = 0.5 * (cheb_high - cheb_low)
    rho_first = radius / centre
    rho_next = 1.0 / (2.0 * centre / radius - rho_first)
    update = setup["dinv"] * rhs / centre
    iterate = update
    remainder = rhs - operate(iterate)
    update = rho_next * rho_first * update + 2.0 * rho_next / radius * setup["dinv"] * remainder
    return iterate + update


def restrict(setup, values):
    pick_lanes = setup["prolong_lanes"]
    blocks = setup["prolong_blocks"]
    coarse_points = pick_lanes.shape[1]
    step_one = jnp.sum(pick_lanes[:, :, None, :] * values[:, None, :, :], axis=0)
    step_two = jnp.sum(pick_lanes[None, :, :, :] * step_one[:, :, None, :], axis=1)
    grouped = step_two.reshape(coarse_points, coarse_points, blocks.shape[0], -1)
    return jnp.einsum("abgq,gqr->abgr", grouped, blocks, precision=precise).reshape(
        coarse_points, coarse_points, -1
    )


def prolong(setup, values):
    pick_lanes = setup["prolong_lanes"]
    blocks = setup["prolong_blocks"]
    coarse_points = pick_lanes.shape[1]
    grouped = values.reshape(coarse_points, coarse_points, blocks.shape[0], -1)
    step_one = jnp.einsum("abgr,gqr->abgq", grouped, blocks, precision=precise).reshape(
        coarse_points, coarse_points, -1
    )
    step_two = jnp.sum(pick_lanes[None, :, :, :] * step_one[:, None, :, :], axis=2)
    return jnp.sum(pick_lanes[:, :, None, :] * step_two[None, :, :, :], axis=1)


def vcycle(fine_rhs, levels, operate):
    fine_op = functools.partial(operate, 0)
    middle_op = functools.partial(operate, 1)
    coarse_op = functools.partial(operate, 2)
    fine_x = smooth(fine_rhs, levels[0], fine_op)
    middle_rhs = restrict(levels[0], fine_rhs - fine_op(fine_x))
    middle_x = smooth(middle_rhs, levels[1], middle_op)
    coarse_rhs = restrict(levels[1], middle_rhs - middle_op(middle_x))
    coarse_x = smooth(coarse_rhs, levels[2], coarse_op)
    coarse_x = coarse_x + smooth(coarse_rhs - coarse_op(coarse_x), levels[2], coarse_op)
    middle_x = middle_x + prolong(levels[1], coarse_x)
    middle_x = middle_x + smooth(middle_rhs - middle_op(middle_x), levels[1], middle_op)
    fine_x = fine_x + prolong(levels[0], middle_x)
    return fine_x + smooth(fine_rhs - fine_op(fine_x), levels[0], fine_op)


def neighbours(own_traces, row_count, layer_count, strip_width):
    points = own_traces[0].shape[1]
    face_size = points * points
    grid = [trace.reshape(row_count, layer_count, face_size) for trace in own_traces]
    layer_index = jnp.arange(layer_count)
    last_layer = (layer_index == strip_width - 1).astype(jnp.float32)
    x_faces = jnp.stack([grid[0], grid[1]])
    z_faces = jnp.stack([grid[4][:, 0], jnp.sum(grid[5] * last_layer[None, :, None], axis=1)])
    x_halo = with_halo(x_faces, (("dom", 0),), 1)
    z_halo = with_halo(z_faces, (("grp", 0),), 1)
    from_prev_x = x_halo[0]
    from_next_x = x_halo[3]
    from_prev_z = z_halo[0]
    from_next_z = z_halo[3]
    zero_row = jnp.zeros_like(grid[0][:1])
    below = jnp.concatenate([zero_row, grid[3][:-1]], axis=0)
    above = jnp.concatenate([grid[2][1:], zero_row], axis=0)
    zero_layer = jnp.zeros_like(grid[0][:, :1])
    behind = jnp.where(
        layer_index[None, :, None] == 0,
        from_prev_z[:, None, :],
        jnp.concatenate([zero_layer, grid[5][:, :-1]], axis=1),
    )
    ahead = jnp.where(
        layer_index[None, :, None] + 1 < strip_width,
        jnp.concatenate([grid[4][:, 1:], zero_layer], axis=1),
        from_next_z[:, None, :],
    )
    nearby = [from_prev_x, from_next_x, below, above, behind, ahead]
    return [entry.reshape(-1, points, points) for entry in nearby]


def strip_cycle(field, strip_orders, strip_factors, layer_alive, strip_width):
    row_count = field.shape[0]
    layer_count = field.shape[1]
    elements = row_count * layer_count
    element_mask = jnp.broadcast_to(layer_alive[None, :], (row_count, layer_count)).reshape(-1)
    levels = build_levels(strip_orders.reshape(-1), strip_factors.reshape(-1, 4), element_mask)

    def operate(level_index, values):
        setup = levels[level_index]
        own_traces = traces(values, setup)
        nearby = neighbours(own_traces, row_count, layer_count, strip_width)
        applied = volume(values, setup) + face_apply(setup, own_traces, nearby)
        return applied * setup["mask_lanes"]

    lanes_rhs = jnp.transpose(field.reshape(elements, 16, 16, 16), (1, 2, 0, 3)).reshape(
        16, 16, elements * 16
    )
    fine_rhs = lanes_rhs * levels[0]["node_live"]
    result = vcycle(fine_rhs, levels, operate)
    back = jnp.transpose(result.reshape(16, 16, elements, 16), (2, 0, 1, 3))
    return back.reshape(row_count, layer_count, -1)


def shards(residual, orders, factors, widths):
    groups = lax.axis_size("grp")
    my_group = lax.axis_index("grp")
    slot_count = residual.shape[2]
    group_ids = jnp.arange(groups)
    my_width = jnp.sum(jnp.where(group_ids == my_group, widths, 0))
    slot_alive = (jnp.arange(slot_count) < my_width).astype(jnp.float32)
    output = strip_cycle(residual[0], orders[0], factors[0], slot_alive, my_width)
    return output[None]


def solution(mesh):
    return jax.shard_map(
        shards,
        mesh=mesh,
        in_specs=(
            P("dom", None, "grp", None),
            P("dom", None, "grp"),
            P("dom", None, "grp", None),
            P(),
        ),
        out_specs=P("dom", None, "grp", None),
        check_vma=False,
    )
```

profile of v0, /device:TPU:24, one launch (start us, length us, event | category | flops | bytes accessed | tf_op | source)
XLA Modules:
  0.0 411.3 jit_solution(17513249056667668261)
XLA Ops:
  4.1 2.3 copy.1953
  6.4 2.4 reshape.1850
  18.7 2.6 collective-permute-start.3
  23.4 14.0 %collective-permute-start.2 = (f32[1,4,256]{2,1,0:T(4,128)}, f32[1,4,256]{2,1,0:T(4,128)}, u32[]{:S(2)}, u32[]{:S(2)}) collective-permute-start(f32[1,4,256]{2,1,0:T(4,128)} %bitcast.27), channel_id=1, source_target_pairs={{0,1},{1,2},{2,3},{3,0},{4,5},{5,6},{6,7},{7,4},{8,9},{9,10},{10,1... | collective-permute-start | bytes 12296 | tf_op jit(solution)/shard_map/ppermute | solution.py:22
  38.9 10.1 %collective-permute-start.1 = (f32[1,4,3,256]{3,2,1,0:T(4,128)}, f32[1,4,3,256]{3,2,1,0:T(4,128)}, u32[]{:S(2)}, u32[]{:S(2)}) collective-permute-start(f32[1,4,3,256]{3,2,1,0:T(4,128)} %stack_reshape.67), channel_id=1, source_target_pairs={{4,0},{8,4},{12,8},{16,12},{20,16},{24,20},{28,24},{32,28},{36,32}... | collective-permute-start | bytes 36872 | tf_op jit(solution)/shard_map/ppermute | solution.py:25
  49.3 4.1 multiply_reduce_fusion.11
  54.6 2.1 collective-permute-start
  66.6 1.5 broadcast_multiply_fusion
  71.3 2.0 multiply_reduce_fusion.7
  86.6 1.3 mul.4627
  105.5 1.5 fusion.373
  110.2 2.1 fusion.21
  143.5 1.9 collective-permute-start.7
  145.7 5.1 %collective-permute-start.6 = (f32[1,4,256]{2,1,0:T(4,128)S(1)}, f32[1,4,256]{2,1,0:T(4,128)S(1)}, u32[]{:S(2)}, u32[]{:S(2)}) collective-permute-start(f32[1,4,256]{2,1,0:T(4,128)S(1)} %bitcast.1239), channel_id=1, source_target_pairs={{0,1},{1,2},{2,3},{3,0},{4,5},{5,6},{6,7},{7,4},{8,9},{9,10},{10,1... | collective-permute-start | bytes 12296 | tf_op jit(solution)/shard_map/ppermute | solution.py:22
  154.5 6.4 %collective-permute-start.5 = (f32[1,4,3,256]{3,2,1,0:T(4,128)S(1)}, f32[1,4,3,256]{3,2,1,0:T(4,128)S(1)}, u32[]{:S(2)}, u32[]{:S(2)}) collective-permute-start(f32[1,4,3,256]{3,2,1,0:T(4,128)S(1)} %stack_reshape.69), channel_id=1, source_target_pairs={{4,0},{8,4},{12,8},{16,12},{20,16},{24,20},{28,24},{32,28},{36,32}... | collective-permute-start | bytes 36872 | tf_op jit(solution)/shard_map/ppermute | solution.py:25
  162.1 2.3 collective-permute-start.4
  166.7 3.8 collective-permute-done.4
  174.2 1.9 collective-permute-start.11
  176.3 5.1 %collective-permute-start.10 = (f32[1,4,64]{2,1,0:T(4,128)S(1)}, f32[1,4,64]{2,1,0:T(4,128)S(1)}, u32[]{:S(2)}, u32[]{:S(2)}) collective-permute-start(f32[1,4,64]{2,1,0:T(4,128)S(1)} %bitcast.1258), channel_id=1, source_target_pairs={{0,1},{1,2},{2,3},{3,0},{4,5},{5,6},{6,7},{7,4},{8,9},{9,10},{10,1... | collective-permute-start | bytes 3080 | tf_op jit(solution)/shard_map/ppermute | solution.py:22
  184.8 2.6 collective-permute-start.9
  188.3 1.9 collective-permute-start.8
  192.4 4.2 %collective-permute-done.8 = f32[1,4,3,64]{3,2,1,0:T(4,128)S(1)} collective-permute-done((f32[1,4,3,64]{3,2,1,0:T(4,128)S(1)}, f32[1,4,3,64]{3,2,1,0:T(4,128)S(1)}, u32[]{:S(2)}, u32[]{:S(2)}) %collective-permute-start.8) | collective-permute-done | bytes 3104 | tf_op jit(solution)/shard_map/ppermute | solution.py:22
  199.1 1.9 collective-permute-start.15
  201.2 5.1 %collective-permute-start.14 = (f32[1,4,64]{2,1,0:T(4,128)S(1)}, f32[1,4,64]{2,1,0:T(4,128)S(1)}, u32[]{:S(2)}, u32[]{:S(2)}) collective-permute-start(f32[1,4,64]{2,1,0:T(4,128)S(1)} %bitcast.1259), channel_id=1, source_target_pairs={{0,1},{1,2},{2,3},{3,0},{4,5},{5,6},{6,7},{7,4},{8,9},{9,10},{10,1... | collective-permute-start | bytes 3080 | tf_op jit(solution)/shard_map/ppermute | solution.py:22
  209.7 2.2 collective-permute-start.13
  212.9 2.3 collective-permute-start.12
  217.4 3.8 collective-permute-done.12
  224.3 1.9 collective-permute-start.19
  226.5 5.1 %collective-permute-start.18 = (f32[1,4,4]{2,1,0:T(4,128)S(1)}, f32[1,4,4]{2,1,0:T(4,128)S(1)}, u32[]{:S(2)}, u32[]{:S(2)}) collective-permute-start(f32[1,4,4]{2,1,0:T(4,128)S(1)} %bitcast.1244), channel_id=1, source_target_pairs={{0,1},{1,2},{2,3},{3,0},{4,5},{5,6},{6,7},{7,4},{8,9},{9,10},{10,1... | collective-permute-start | bytes 200 | tf_op jit(solution)/shard_map/ppermute | solution.py:22
  235.9 2.5 collective-permute-start.17
  238.8 1.9 collective-permute-start.16
  243.3 3.8 collective-permute-done.16
  249.8 1.9 collective-permute-start.23
  252.1 5.1 %collective-permute-start.22 = (f32[1,4,4]{2,1,0:T(4,128)S(1)}, f32[1,4,4]{2,1,0:T(4,128)S(1)}, u32[]{:S(2)}, u32[]{:S(2)}) collective-permute-start(f32[1,4,4]{2,1,0:T(4,128)S(1)} %bitcast.1249), channel_id=1, source_target_pairs={{0,1},{1,2},{2,3},{3,0},{4,5},{5,6},{6,7},{7,4},{8,9},{9,10},{10,1... | collective-permute-start | bytes 200 | tf_op jit(solution)/shard_map/ppermute | solution.py:22
  261.5 2.6 collective-permute-start.21
  264.4 1.9 collective-permute-start.20
  268.9 3.8 collective-permute-done.20
  275.5 1.9 collective-permute-start.27
  277.8 5.3 %collective-permute-start.26 = (f32[1,4,4]{2,1,0:T(4,128)S(1)}, f32[1,4,4]{2,1,0:T(4,128)S(1)}, u32[]{:S(2)}, u32[]{:S(2)}) collective-permute-start(f32[1,4,4]{2,1,0:T(4,128)S(1)} %bitcast.1246), channel_id=1, source_target_pairs={{0,1},{1,2},{2,3},{3,0},{4,5},{5,6},{6,7},{7,4},{8,9},{9,10},{10,1... | collective-permute-start | bytes 200 | tf_op jit(solution)/shard_map/ppermute | solution.py:22
  287.3 2.6 collective-permute-start.25
  290.3 1.9 collective-permute-start.24
  294.8 3.8 collective-permute-done.24
  301.4 1.9 collective-permute-start.31
  303.5 5.1 %collective-permute-start.30 = (f32[1,4,64]{2,1,0:T(4,128)S(1)}, f32[1,4,64]{2,1,0:T(4,128)S(1)}, u32[]{:S(2)}, u32[]{:S(2)}) collective-permute-start(f32[1,4,64]{2,1,0:T(4,128)S(1)} %bitcast.1260), channel_id=1, source_target_pairs={{0,1},{1,2},{2,3},{3,0},{4,5},{5,6},{6,7},{7,4},{8,9},{9,10},{10,1... | collective-permute-start | bytes 3080 | tf_op jit(solution)/shard_map/ppermute | solution.py:22
  312.0 2.7 collective-permute-start.29
  315.4 1.9 collective-permute-start.28
  319.6 4.2 %collective-permute-done.28 = f32[1,4,3,64]{3,2,1,0:T(4,128)S(1)} collective-permute-done((f32[1,4,3,64]{3,2,1,0:T(4,128)S(1)}, f32[1,4,3,64]{3,2,1,0:T(4,128)S(1)}, u32[]{:S(2)}, u32[]{:S(2)}) %collective-permute-start.28) | collective-permute-done | bytes 3104 | tf_op jit(solution)/shard_map/ppermute | solution.py:22
  326.3 1.9 collective-permute-start.35
  328.4 5.1 %collective-permute-start.34 = (f32[1,4,64]{2,1,0:T(4,128)S(1)}, f32[1,4,64]{2,1,0:T(4,128)S(1)}, u32[]{:S(2)}, u32[]{:S(2)}) collective-permute-start(f32[1,4,64]{2,1,0:T(4,128)S(1)} %bitcast.1257), channel_id=1, source_target_pairs={{0,1},{1,2},{2,3},{3,0},{4,5},{5,6},{6,7},{7,4},{8,9},{9,10},{10,1... | collective-permute-start | bytes 3080 | tf_op jit(solution)/shard_map/ppermute | solution.py:22
  336.9 2.2 collective-permute-start.33
  339.9 2.5 collective-permute-start.32
  344.6 3.6 collective-permute-done.32
  353.2 1.9 collective-permute-start.39
  355.3 5.1 %collective-permute-start.38 = (f32[1,4,256]{2,1,0:T(4,128)S(1)}, f32[1,4,256]{2,1,0:T(4,128)S(1)}, u32[]{:S(2)}, u32[]{:S(2)}) collective-permute-start(f32[1,4,256]{2,1,0:T(4,128)S(1)} %bitcast.1240), channel_id=1, source_target_pairs={{0,1},{1,2},{2,3},{3,0},{4,5},{5,6},{6,7},{7,4},{8,9},{9,10},{10,1... | collective-permute-start | bytes 12296 | tf_op jit(solution)/shard_map/ppermute | solution.py:22
  364.2 2.6 collective-permute-start.37
  368.0 2.1 collective-permute-start.36
  372.2 4.2 %collective-permute-done.36 = f32[1,4,3,256]{3,2,1,0:T(4,128)S(1)} collective-permute-done((f32[1,4,3,256]{3,2,1,0:T(4,128)S(1)}, f32[1,4,3,256]{3,2,1,0:T(4,128)S(1)}, u32[]{:S(2)}, u32[]{:S(2)}) %collective-permute-start.36) | collective-permute-done | bytes 12320 | tf_op jit(solution)/shard_map/ppermute | solution.py:22
  381.3 1.9 collective-permute-start.43
  383.5 5.1 %collective-permute-start.42 = (f32[1,4,256]{2,1,0:T(4,128)S(1)}, f32[1,4,256]{2,1,0:T(4,128)S(1)}, u32[]{:S(2)}, u32[]{:S(2)}) collective-permute-start(f32[1,4,256]{2,1,0:T(4,128)S(1)} %bitcast.1238), channel_id=1, source_target_pairs={{0,1},{1,2},{2,3},{3,0},{4,5},{5,6},{6,7},{7,4},{8,9},{9,10},{10,1... | collective-permute-start | bytes 12296 | tf_op jit(solution)/shard_map/ppermute | solution.py:22
  392.3 2.2 collective-permute-start.41
  395.7 2.3 collective-permute-start.40
  400.1 4.0 collective-permute-done.40
  406.3 1.7 copy.2423
  408.0 2.3 broadcast_in_dim_reshape.11
  (1403 shorter events, 193.6 us)
Async XLA Ops:
  0.0 63.4 %copy-start.80 = (s32[9]{0:T(128)}, s32[9]{0:T(128)S(1)}, u32[]{:S(2)}) copy-start(s32[9]{0:T(128)S(1)} %iota_add_fusion) | copy-start | bytes 112
  0.9 62.5 %copy-start.71 = (s32[12]{0:T(128)}, s32[12]{0:T(128)S(1)}, u32[]{:S(2)}) copy-start(s32[12]{0:T(128)S(1)} %eq.127) | copy-start | bytes 148
  10.1 39.1 %copy-start.83 = (f32[12]{0:T(128)}, f32[12]{0:T(128)S(1)}, u32[]{:S(2)}) copy-start(f32[12]{0:T(128)S(1)} %reshape.1849) | copy-start | bytes 148
  12.6 36.5 %copy-start.86 = (f32[12]{0:T(128)}, f32[12]{0:T(128)S(1)}, u32[]{:S(2)}) copy-start(f32[12]{0:T(128)S(1)} %get-tuple-element.104) | copy-start | bytes 148
  12.6 36.5 %copy-start.88 = (f32[12]{0:T(128)}, f32[12]{0:T(128)S(1)}, u32[]{:S(2)}) copy-start(f32[12]{0:T(128)S(1)} %get-tuple-element.103) | copy-start | bytes 148
  12.6 36.5 %copy-start.90 = (f32[12]{0:T(128)}, f32[12]{0:T(128)S(1)}, u32[]{:S(2)}) copy-start(f32[12]{0:T(128)S(1)} %get-tuple-element.102) | copy-start | bytes 148
  12.6 36.5 %copy-start.92 = (f32[12]{0:T(128)}, f32[12]{0:T(128)S(1)}, u32[]{:S(2)}) copy-start(f32[12]{0:T(128)S(1)} %get-tuple-element.105) | copy-start | bytes 148
  16.0 94.2 %copy-start.16 = (f32[16,192]{1,0:T(8,128)}, f32[16,192]{1,0:T(8,128)S(1)}, u32[]{:S(2)}) copy-start(f32[16,192]{1,0:T(8,128)S(1)} %get-tuple-element.60) | copy-start | bytes 36868
  18.7 114.6 %collective-permute-start.3 = (f32[1,4,256]{2,0,1:T(1,128)}, f32[1,4,256]{2,0,1:T(1,128)}, u32[]{:S(2)}, u32[]{:S(2)}) collective-permute-start(f32[1,4,256]{2,0,1:T(1,128)} %slice_bitcast_fusion.19), channel_id=1, source_target_pairs={{1,0},{2,1},{3,2},{0,3},{5,4},{6,5},{7,6},{4,7},{9,8},{10,9},{11,1... | collective-permute-start | bytes 12296 | tf_op jit(solution)/shard_map/ppermute | solution.py:25
  22.2 31.2 %copy-start.39 = (f32[4,3,256]{2,1,0:T(4,128)}, f32[4,3,256]{2,1,0:T(4,128)S(1)}, u32[]{:S(2)}) copy-start(f32[4,3,256]{2,1,0:T(4,128)S(1)} %reshape.1854) | copy-start | bytes 36868
  23.4 111.3 %collective-permute-start.2 = (f32[1,4,256]{2,1,0:T(4,128)}, f32[1,4,256]{2,1,0:T(4,128)}, u32[]{:S(2)}, u32[]{:S(2)}) collective-permute-start(f32[1,4,256]{2,1,0:T(4,128)} %bitcast.27), channel_id=1, source_target_pairs={{0,1},{1,2},{2,3},{3,0},{4,5},{5,6},{6,7},{7,4},{8,9},{9,10},{10,1... | collective-permute-start | bytes 12296 | tf_op jit(solution)/shard_map/ppermute | solution.py:22
  38.9 97.4 %collective-permute-start.1 = (f32[1,4,3,256]{3,2,1,0:T(4,128)}, f32[1,4,3,256]{3,2,1,0:T(4,128)}, u32[]{:S(2)}, u32[]{:S(2)}) collective-permute-start(f32[1,4,3,256]{3,2,1,0:T(4,128)} %stack_reshape.67), channel_id=1, source_target_pairs={{4,0},{8,4},{12,8},{16,12},{20,16},{24,20},{28,24},{32,28},{36,32}... | collective-permute-start | bytes 36872 | tf_op jit(solution)/shard_map/ppermute | solution.py:25
  54.6 83.1 %collective-permute-start = (f32[1,4,3,256]{3,2,1,0:T(4,128)}, f32[1,4,3,256]{3,2,1,0:T(4,128)}, u32[]{:S(2)}, u32[]{:S(2)}) collective-permute-start(f32[1,4,3,256]{3,2,1,0:T(4,128)} %stack_reshape.66), channel_id=1, source_target_pairs={{0,4},{4,8},{8,12},{12,16},{16,20},{20,24},{24,28},{28,32},{32,36}... | collective-permute-start | bytes 36872 | tf_op jit(solution)/shard_map/ppermute | solution.py:22
  65.8 41.2 %copy-start.14 = (f32[16,192]{1,0:T(8,128)}, f32[16,192]{1,0:T(8,128)S(1)}, u32[]{:S(2)}) copy-start(f32[16,192]{1,0:T(8,128)S(1)} %mul.4399) | copy-start | bytes 36868
  77.2 33.0 %copy-start.18 = (f32[16,192]{1,0:T(8,128)S(1)}, f32[16,192]{1,0:T(8,128)}, u32[]{:S(2)}) copy-start(f32[16,192]{1,0:T(8,128)} %get-tuple-element.79) | copy-start | bytes 36868
  79.8 32.6 %copy-start.37 = (f32[8,96]{1,0:T(8,128)}, f32[8,96]{1,0:T(8,128)S(1)}, u32[]{:S(2)}) copy-start(f32[8,96]{1,0:T(8,128)S(1)} %mul.4452) | copy-start | bytes 9220
  83.2 29.1 %copy-start.51 = (f32[8,12]{1,0:T(8,128)}, f32[8,12]{1,0:T(8,128)S(1)}, u32[]{:S(2)}) copy-start(f32[8,12]{1,0:T(8,128)S(1)} %gather_fusion.1) | copy-start | bytes 1156
  85.8 28.5 %copy-start.62 = (f32[4,3,256]{2,1,0:T(4,128)S(1)}, f32[4,3,256]{2,1,0:T(4,128)}, u32[]{:S(2)}) copy-start(f32[4,3,256]{2,1,0:T(4,128)} %copy-done.61) | copy-start | bytes 36868
  114.3 50.8 %copy-start.56 = (pred[3]{0:T(512)(128)(4,1)}, pred[3]{0:T(512)(128)(4,1)S(1)}, u32[]{:S(2)}) copy-start(pred[3]{0:T(512)(128)(4,1)S(1)} %iota_compare_fusion.1) | copy-start | bytes 13
  143.5 20.9 %collective-permute-start.7 = (f32[1,4,256]{2,0,1:T(1,128)S(1)}, f32[1,4,256]{2,0,1:T(1,128)S(1)}, u32[]{:S(2)}, u32[]{:S(2)}) collective-permute-start(f32[1,4,256]{2,0,1:T(1,128)S(1)} %slice_bitcast_fusion.18), channel_id=1, source_target_pairs={{1,0},{2,1},{3,2},{0,3},{5,4},{6,5},{7,6},{4,7},{9,8},{10,9},{11,1... | collective-permute-start | bytes 12296 | tf_op jit(solution)/shard_map/ppermute | solution.py:25
  145.7 19.4 %collective-permute-start.6 = (f32[1,4,256]{2,1,0:T(4,128)S(1)}, f32[1,4,256]{2,1,0:T(4,128)S(1)}, u32[]{:S(2)}, u32[]{:S(2)}) collective-permute-start(f32[1,4,256]{2,1,0:T(4,128)S(1)} %bitcast.1239), channel_id=1, source_target_pairs={{0,1},{1,2},{2,3},{3,0},{4,5},{5,6},{6,7},{7,4},{8,9},{9,10},{10,1... | collective-permute-start | bytes 12296 | tf_op jit(solution)/shard_map/ppermute | solution.py:22
  154.5 11.3 %collective-permute-start.5 = (f32[1,4,3,256]{3,2,1,0:T(4,128)S(1)}, f32[1,4,3,256]{3,2,1,0:T(4,128)S(1)}, u32[]{:S(2)}, u32[]{:S(2)}) collective-permute-start(f32[1,4,3,256]{3,2,1,0:T(4,128)S(1)} %stack_reshape.69), channel_id=1, source_target_pairs={{4,0},{8,4},{12,8},{16,12},{20,16},{24,20},{28,24},{32,28},{36,32}... | collective-permute-start | bytes 36872 | tf_op jit(solution)/shard_map/ppermute | solution.py:25
  162.1 8.4 %collective-permute-start.4 = (f32[1,4,3,256]{3,2,1,0:T(4,128)S(1)}, f32[1,4,3,256]{3,2,1,0:T(4,128)S(1)}, u32[]{:S(2)}, u32[]{:S(2)}) collective-permute-start(f32[1,4,3,256]{3,2,1,0:T(4,128)S(1)} %stack_reshape.68), channel_id=1, source_target_pairs={{0,4},{4,8},{8,12},{12,16},{16,20},{20,24},{24,28},{28,32},{32,36}... | collective-permute-start | bytes 36872 | tf_op jit(solution)/shard_map/ppermute | solution.py:22
  174.2 16.0 %collective-permute-start.11 = (f32[1,4,64]{2,1,0:T(4,128)S(1)}, f32[1,4,64]{2,1,0:T(4,128)S(1)}, u32[]{:S(2)}, u32[]{:S(2)}) collective-permute-start(f32[1,4,64]{2,1,0:T(4,128)S(1)} %bitcast.1254), channel_id=1, source_target_pairs={{1,0},{2,1},{3,2},{0,3},{5,4},{6,5},{7,6},{4,7},{9,8},{10,9},{11,1... | collective-permute-start | bytes 3080 | tf_op jit(solution)/shard_map/ppermute | solution.py:25
  176.3 14.5 %collective-permute-start.10 = (f32[1,4,64]{2,1,0:T(4,128)S(1)}, f32[1,4,64]{2,1,0:T(4,128)S(1)}, u32[]{:S(2)}, u32[]{:S(2)}) collective-permute-start(f32[1,4,64]{2,1,0:T(4,128)S(1)} %bitcast.1258), channel_id=1, source_target_pairs={{0,1},{1,2},{2,3},{3,0},{4,5},{5,6},{6,7},{7,4},{8,9},{9,10},{10,1... | collective-permute-start | bytes 3080 | tf_op jit(solution)/shard_map/ppermute | solution.py:22
  184.8 6.9 %collective-permute-start.9 = (f32[1,4,3,64]{3,2,1,0:T(4,128)S(1)}, f32[1,4,3,64]{3,2,1,0:T(4,128)S(1)}, u32[]{:S(2)}, u32[]{:S(2)}) collective-permute-start(f32[1,4,3,64]{3,2,1,0:T(4,128)S(1)} %stack_reshape.71), channel_id=1, source_target_pairs={{4,0},{8,4},{12,8},{16,12},{20,16},{24,20},{28,24},{32,28},{36,32}... | collective-permute-start | bytes 9224 | tf_op jit(solution)/shard_map/ppermute | solution.py:25
  188.3 8.3 %collective-permute-start.8 = (f32[1,4,3,64]{3,2,1,0:T(4,128)S(1)}, f32[1,4,3,64]{3,2,1,0:T(4,128)S(1)}, u32[]{:S(2)}, u32[]{:S(2)}) collective-permute-start(f32[1,4,3,64]{3,2,1,0:T(4,128)S(1)} %stack_reshape.70), channel_id=1, source_target_pairs={{0,4},{4,8},{8,12},{12,16},{16,20},{20,24},{24,28},{28,32},{32,36}... | collective-permute-start | bytes 9224 | tf_op jit(solution)/shard_map/ppermute | solution.py:22
  199.1 16.0 %collective-permute-start.15 = (f32[1,4,64]{2,1,0:T(4,128)S(1)}, f32[1,4,64]{2,1,0:T(4,128)S(1)}, u32[]{:S(2)}, u32[]{:S(2)}) collective-permute-start(f32[1,4,64]{2,1,0:T(4,128)S(1)} %bitcast.1255), channel_id=1, source_target_pairs={{1,0},{2,1},{3,2},{0,3},{5,4},{6,5},{7,6},{4,7},{9,8},{10,9},{11,1... | collective-permute-start | bytes 3080 | tf_op jit(solution)/shard_map/ppermute | solution.py:25
  201.2 14.6 %collective-permute-start.14 = (f32[1,4,64]{2,1,0:T(4,128)S(1)}, f32[1,4,64]{2,1,0:T(4,128)S(1)}, u32[]{:S(2)}, u32[]{:S(2)}) collective-permute-start(f32[1,4,64]{2,1,0:T(4,128)S(1)} %bitcast.1259), channel_id=1, source_target_pairs={{0,1},{1,2},{2,3},{3,0},{4,5},{5,6},{6,7},{7,4},{8,9},{9,10},{10,1... | collective-permute-start | bytes 3080 | tf_op jit(solution)/shard_map/ppermute | solution.py:22
  209.7 7.0 %collective-permute-start.13 = (f32[1,4,3,64]{3,2,1,0:T(4,128)S(1)}, f32[1,4,3,64]{3,2,1,0:T(4,128)S(1)}, u32[]{:S(2)}, u32[]{:S(2)}) collective-permute-start(f32[1,4,3,64]{3,2,1,0:T(4,128)S(1)} %stack_reshape.73), channel_id=1, source_target_pairs={{4,0},{8,4},{12,8},{16,12},{20,16},{24,20},{28,24},{32,28},{36,32}... | collective-permute-start | bytes 9224 | tf_op jit(solution)/shard_map/ppermute | solution.py:25
  212.9 8.3 %collective-permute-start.12 = (f32[1,4,3,64]{3,2,1,0:T(4,128)S(1)}, f32[1,4,3,64]{3,2,1,0:T(4,128)S(1)}, u32[]{:S(2)}, u32[]{:S(2)}) collective-permute-start(f32[1,4,3,64]{3,2,1,0:T(4,128)S(1)} %stack_reshape.72), channel_id=1, source_target_pairs={{0,4},{4,8},{8,12},{12,16},{16,20},{20,24},{24,28},{28,32},{32,36}... | collective-permute-start | bytes 9224 | tf_op jit(solution)/shard_map/ppermute | solution.py:22
  216.2 22.3 %copy-start.94 = (f32[24,24,1]{1,0,2:T(8,128)S(1)}, f32[24,24,1]{1,0,2:T(8,128)}, u32[]{:S(2)}) copy-start(f32[24,24,1]{1,0,2:T(8,128)} %reshape.1984) | copy-start | bytes 6916
  216.3 22.3 %copy-start.148 = (f32[2,24]{1,0:T(2,128)S(1)}, f32[2,24]{1,0:T(2,128)}, u32[]{:S(2)}) copy-start(f32[2,24]{1,0:T(2,128)} %get-tuple-element.55) | copy-start | bytes 580
  216.6 24.2 %copy-start.55 = (pred[3]{0:T(512)(128)(4,1)S(1)}, pred[3]{0:T(512)(128)(4,1)}, u32[]{:S(2)}) copy-start(pred[3]{0:T(512)(128)(4,1)} %add_compare_fusion) | copy-start | bytes 13
  217.4 30.4 %copy-start.127 = (f32[2,24]{1,0:T(2,128)S(1)}, f32[2,24]{1,0:T(2,128)}, u32[]{:S(2)}) copy-start(f32[2,24]{1,0:T(2,128)} %copy-done.126) | copy-start | bytes 580
  217.4 30.4 %copy-start.137 = (f32[2]{0:T(128)S(1)}, f32[2]{0:T(128)}, u32[]{:S(2)}) copy-start(f32[2]{0:T(128)} %constant.146.clone) | copy-start | bytes 28
  224.3 16.4 %collective-permute-start.19 = (f32[1,4,4]{2,1,0:T(4,128)S(1)}, f32[1,4,4]{2,1,0:T(4,128)S(1)}, u32[]{:S(2)}, u32[]{:S(2)}) collective-permute-start(f32[1,4,4]{2,1,0:T(4,128)S(1)} %bitcast.1241), channel_id=1, source_target_pairs={{1,0},{2,1},{3,2},{0,3},{5,4},{6,5},{7,6},{4,7},{9,8},{10,9},{11,1... | collective-permute-start | bytes 200 | tf_op jit(solution)/shard_map/ppermute | solution.py:25
  226.5 15.0 %collective-permute-start.18 = (f32[1,4,4]{2,1,0:T(4,128)S(1)}, f32[1,4,4]{2,1,0:T(4,128)S(1)}, u32[]{:S(2)}, u32[]{:S(2)}) collective-permute-start(f32[1,4,4]{2,1,0:T(4,128)S(1)} %bitcast.1244), channel_id=1, source_target_pairs={{0,1},{1,2},{2,3},{3,0},{4,5},{5,6},{6,7},{7,4},{8,9},{9,10},{10,1... | collective-permute-start | bytes 200 | tf_op jit(solution)/shard_map/ppermute | solution.py:22
  235.9 6.6 %collective-permute-start.17 = (f32[1,4,3,4]{2,1,3,0:T(4,128)S(1)}, f32[1,4,3,4]{2,1,3,0:T(4,128)S(1)}, u32[]{:S(2)}, u32[]{:S(2)}) collective-permute-start(f32[1,4,3,4]{2,1,3,0:T(4,128)S(1)} %stack_reshape.75), channel_id=1, source_target_pairs={{4,0},{8,4},{12,8},{16,12},{20,16},{24,20},{28,24},{32,28},{36,32}... | collective-permute-start | bytes 584 | tf_op jit(solution)/shard_map/ppermute | solution.py:25
  238.8 8.3 %collective-permute-start.16 = (f32[1,4,3,4]{2,1,3,0:T(4,128)S(1)}, f32[1,4,3,4]{2,1,3,0:T(4,128)S(1)}, u32[]{:S(2)}, u32[]{:S(2)}) collective-permute-start(f32[1,4,3,4]{2,1,3,0:T(4,128)S(1)} %stack_reshape.74), channel_id=1, source_target_pairs={{0,4},{4,8},{8,12},{12,16},{16,20},{20,24},{24,28},{28,32},{32,36}... | collective-permute-start | bytes 584 | tf_op jit(solution)/shard_map/ppermute | solution.py:22
  249.8 16.5 %collective-permute-start.23 = (f32[1,4,4]{2,1,0:T(4,128)S(1)}, f32[1,4,4]{2,1,0:T(4,128)S(1)}, u32[]{:S(2)}, u32[]{:S(2)}) collective-permute-start(f32[1,4,4]{2,1,0:T(4,128)S(1)} %bitcast.1243), channel_id=1, source_target_pairs={{1,0},{2,1},{3,2},{0,3},{5,4},{6,5},{7,6},{4,7},{9,8},{10,9},{11,1... | collective-permute-start | bytes 200 | tf_op jit(solution)/shard_map/ppermute | solution.py:25
  252.1 15.1 %collective-permute-start.22 = (f32[1,4,4]{2,1,0:T(4,128)S(1)}, f32[1,4,4]{2,1,0:T(4,128)S(1)}, u32[]{:S(2)}, u32[]{:S(2)}) collective-permute-start(f32[1,4,4]{2,1,0:T(4,128)S(1)} %bitcast.1249), channel_id=1, source_target_pairs={{0,1},{1,2},{2,3},{3,0},{4,5},{5,6},{6,7},{7,4},{8,9},{9,10},{10,1... | collective-permute-start | bytes 200 | tf_op jit(solution)/shard_map/ppermute | solution.py:22
  261.5 6.7 %collective-permute-start.21 = (f32[1,4,3,4]{2,1,3,0:T(4,128)S(1)}, f32[1,4,3,4]{2,1,3,0:T(4,128)S(1)}, u32[]{:S(2)}, u32[]{:S(2)}) collective-permute-start(f32[1,4,3,4]{2,1,3,0:T(4,128)S(1)} %stack_reshape.77), channel_id=1, source_target_pairs={{4,0},{8,4},{12,8},{16,12},{20,16},{24,20},{28,24},{32,28},{36,32}... | collective-permute-start | bytes 584 | tf_op jit(solution)/shard_map/ppermute | solution.py:25
  264.4 8.3 %collective-permute-start.20 = (f32[1,4,3,4]{2,1,3,0:T(4,128)S(1)}, f32[1,4,3,4]{2,1,3,0:T(4,128)S(1)}, u32[]{:S(2)}, u32[]{:S(2)}) collective-permute-start(f32[1,4,3,4]{2,1,3,0:T(4,128)S(1)} %stack_reshape.76), channel_id=1, source_target_pairs={{0,4},{4,8},{8,12},{12,16},{16,20},{20,24},{24,28},{28,32},{32,36}... | collective-permute-start | bytes 584 | tf_op jit(solution)/shard_map/ppermute | solution.py:22
  275.5 16.7 %collective-permute-start.27 = (f32[1,4,4]{2,1,0:T(4,128)S(1)}, f32[1,4,4]{2,1,0:T(4,128)S(1)}, u32[]{:S(2)}, u32[]{:S(2)}) collective-permute-start(f32[1,4,4]{2,1,0:T(4,128)S(1)} %bitcast.1242), channel_id=1, source_target_pairs={{1,0},{2,1},{3,2},{0,3},{5,4},{6,5},{7,6},{4,7},{9,8},{10,9},{11,1... | collective-permute-start | bytes 200 | tf_op jit(solution)/shard_map/ppermute | solution.py:25
  277.8 15.3 %collective-permute-start.26 = (f32[1,4,4]{2,1,0:T(4,128)S(1)}, f32[1,4,4]{2,1,0:T(4,128)S(1)}, u32[]{:S(2)}, u32[]{:S(2)}) collective-permute-start(f32[1,4,4]{2,1,0:T(4,128)S(1)} %bitcast.1246), channel_id=1, source_target_pairs={{0,1},{1,2},{2,3},{3,0},{4,5},{5,6},{6,7},{7,4},{8,9},{9,10},{10,1... | collective-permute-start | bytes 200 | tf_op jit(solution)/shard_map/ppermute | solution.py:22
  287.3 6.7 %collective-permute-start.25 = (f32[1,4,3,4]{2,1,3,0:T(4,128)S(1)}, f32[1,4,3,4]{2,1,3,0:T(4,128)S(1)}, u32[]{:S(2)}, u32[]{:S(2)}) collective-permute-start(f32[1,4,3,4]{2,1,3,0:T(4,128)S(1)} %stack_reshape.79), channel_id=1, source_target_pairs={{4,0},{8,4},{12,8},{16,12},{20,16},{24,20},{28,24},{32,28},{36,32}... | collective-permute-start | bytes 584 | tf_op jit(solution)/shard_map/ppermute | solution.py:25
  290.3 8.3 %collective-permute-start.24 = (f32[1,4,3,4]{2,1,3,0:T(4,128)S(1)}, f32[1,4,3,4]{2,1,3,0:T(4,128)S(1)}, u32[]{:S(2)}, u32[]{:S(2)}) collective-permute-start(f32[1,4,3,4]{2,1,3,0:T(4,128)S(1)} %stack_reshape.78), channel_id=1, source_target_pairs={{0,4},{4,8},{8,12},{12,16},{16,20},{20,24},{24,28},{28,32},{32,36}... | collective-permute-start | bytes 584 | tf_op jit(solution)/shard_map/ppermute | solution.py:22
  301.4 15.9 %collective-permute-start.31 = (f32[1,4,64]{2,1,0:T(4,128)S(1)}, f32[1,4,64]{2,1,0:T(4,128)S(1)}, u32[]{:S(2)}, u32[]{:S(2)}) collective-permute-start(f32[1,4,64]{2,1,0:T(4,128)S(1)} %bitcast.1256), channel_id=1, source_target_pairs={{1,0},{2,1},{3,2},{0,3},{5,4},{6,5},{7,6},{4,7},{9,8},{10,9},{11,1... | collective-permute-start | bytes 3080 | tf_op jit(solution)/shard_map/ppermute | solution.py:25
  303.5 14.5 %collective-permute-start.30 = (f32[1,4,64]{2,1,0:T(4,128)S(1)}, f32[1,4,64]{2,1,0:T(4,128)S(1)}, u32[]{:S(2)}, u32[]{:S(2)}) collective-permute-start(f32[1,4,64]{2,1,0:T(4,128)S(1)} %bitcast.1260), channel_id=1, source_target_pairs={{0,1},{1,2},{2,3},{3,0},{4,5},{5,6},{6,7},{7,4},{8,9},{9,10},{10,1... | collective-permute-start | bytes 3080 | tf_op jit(solution)/shard_map/ppermute | solution.py:22
  312.0 6.9 %collective-permute-start.29 = (f32[1,4,3,64]{3,2,1,0:T(4,128)S(1)}, f32[1,4,3,64]{3,2,1,0:T(4,128)S(1)}, u32[]{:S(2)}, u32[]{:S(2)}) collective-permute-start(f32[1,4,3,64]{3,2,1,0:T(4,128)S(1)} %stack_reshape.81), channel_id=1, source_target_pairs={{4,0},{8,4},{12,8},{16,12},{20,16},{24,20},{28,24},{32,28},{36,32}... | collective-permute-start | bytes 9224 | tf_op jit(solution)/shard_map/ppermute | solution.py:25
  315.4 8.3 %collective-permute-start.28 = (f32[1,4,3,64]{3,2,1,0:T(4,128)S(1)}, f32[1,4,3,64]{3,2,1,0:T(4,128)S(1)}, u32[]{:S(2)}, u32[]{:S(2)}) collective-permute-start(f32[1,4,3,64]{3,2,1,0:T(4,128)S(1)} %stack_reshape.80), channel_id=1, source_target_pairs={{0,4},{4,8},{8,12},{12,16},{16,20},{20,24},{24,28},{28,32},{32,36}... | collective-permute-start | bytes 9224 | tf_op jit(solution)/shard_map/ppermute | solution.py:22
  326.3 16.1 %collective-permute-start.35 = (f32[1,4,64]{2,1,0:T(4,128)S(1)}, f32[1,4,64]{2,1,0:T(4,128)S(1)}, u32[]{:S(2)}, u32[]{:S(2)}) collective-permute-start(f32[1,4,64]{2,1,0:T(4,128)S(1)} %bitcast.1253), channel_id=1, source_target_pairs={{1,0},{2,1},{3,2},{0,3},{5,4},{6,5},{7,6},{4,7},{9,8},{10,9},{11,1... | collective-permute-start | bytes 3080 | tf_op jit(solution)/shard_map/ppermute | solution.py:25
  328.4 14.6 %collective-permute-start.34 = (f32[1,4,64]{2,1,0:T(4,128)S(1)}, f32[1,4,64]{2,1,0:T(4,128)S(1)}, u32[]{:S(2)}, u32[]{:S(2)}) collective-permute-start(f32[1,4,64]{2,1,0:T(4,128)S(1)} %bitcast.1257), channel_id=1, source_target_pairs={{0,1},{1,2},{2,3},{3,0},{4,5},{5,6},{6,7},{7,4},{8,9},{9,10},{10,1... | collective-permute-start | bytes 3080 | tf_op jit(solution)/shard_map/ppermute | solution.py:22
  336.9 7.1 %collective-permute-start.33 = (f32[1,4,3,64]{3,2,1,0:T(4,128)S(1)}, f32[1,4,3,64]{3,2,1,0:T(4,128)S(1)}, u32[]{:S(2)}, u32[]{:S(2)}) collective-permute-start(f32[1,4,3,64]{3,2,1,0:T(4,128)S(1)} %stack_reshape.83), channel_id=1, source_target_pairs={{4,0},{8,4},{12,8},{16,12},{20,16},{24,20},{28,24},{32,28},{36,32}... | collective-permute-start | bytes 9224 | tf_op jit(solution)/shard_map/ppermute | solution.py:25
  339.9 8.3 %collective-permute-start.32 = (f32[1,4,3,64]{3,2,1,0:T(4,128)S(1)}, f32[1,4,3,64]{3,2,1,0:T(4,128)S(1)}, u32[]{:S(2)}, u32[]{:S(2)}) collective-permute-start(f32[1,4,3,64]{3,2,1,0:T(4,128)S(1)} %stack_reshape.82), channel_id=1, source_target_pairs={{0,4},{4,8},{8,12},{12,16},{16,20},{20,24},{24,28},{28,32},{32,36}... | collective-permute-start | bytes 9224 | tf_op jit(solution)/shard_map/ppermute | solution.py:22
  353.2 16.9 %collective-permute-start.39 = (f32[1,4,256]{2,0,1:T(1,128)S(1)}, f32[1,4,256]{2,0,1:T(1,128)S(1)}, u32[]{:S(2)}, u32[]{:S(2)}) collective-permute-start(f32[1,4,256]{2,0,1:T(1,128)S(1)} %slice_bitcast_fusion.17), channel_id=1, source_target_pairs={{1,0},{2,1},{3,2},{0,3},{5,4},{6,5},{7,6},{4,7},{9,8},{10,9},{11,1... | collective-permute-start | bytes 12296 | tf_op jit(solution)/shard_map/ppermute | solution.py:25
  355.3 15.4 %collective-permute-start.38 = (f32[1,4,256]{2,1,0:T(4,128)S(1)}, f32[1,4,256]{2,1,0:T(4,128)S(1)}, u32[]{:S(2)}, u32[]{:S(2)}) collective-permute-start(f32[1,4,256]{2,1,0:T(4,128)S(1)} %bitcast.1240), channel_id=1, source_target_pairs={{0,1},{1,2},{2,3},{3,0},{4,5},{5,6},{6,7},{7,4},{8,9},{9,10},{10,1... | collective-permute-start | bytes 12296 | tf_op jit(solution)/shard_map/ppermute | solution.py:22
  364.2 7.3 %collective-permute-start.37 = (f32[1,4,3,256]{3,2,1,0:T(4,128)S(1)}, f32[1,4,3,256]{3,2,1,0:T(4,128)S(1)}, u32[]{:S(2)}, u32[]{:S(2)}) collective-permute-start(f32[1,4,3,256]{3,2,1,0:T(4,128)S(1)} %stack_reshape.85), channel_id=1, source_target_pairs={{4,0},{8,4},{12,8},{16,12},{20,16},{24,20},{28,24},{32,28},{36,32}... | collective-permute-start | bytes 36872 | tf_op jit(solution)/shard_map/ppermute | solution.py:25
  368.0 8.4 %collective-permute-start.36 = (f32[1,4,3,256]{3,2,1,0:T(4,128)S(1)}, f32[1,4,3,256]{3,2,1,0:T(4,128)S(1)}, u32[]{:S(2)}, u32[]{:S(2)}) collective-permute-start(f32[1,4,3,256]{3,2,1,0:T(4,128)S(1)} %stack_reshape.84), channel_id=1, source_target_pairs={{0,4},{4,8},{8,12},{12,16},{16,20},{20,24},{24,28},{28,32},{32,36}... | collective-permute-start | bytes 36872 | tf_op jit(solution)/shard_map/ppermute | solution.py:22
  381.3 16.7 %collective-permute-start.43 = (f32[1,4,256]{2,0,1:T(1,128)S(1)}, f32[1,4,256]{2,0,1:T(1,128)S(1)}, u32[]{:S(2)}, u32[]{:S(2)}) collective-permute-start(f32[1,4,256]{2,0,1:T(1,128)S(1)} %slice_bitcast_fusion.16), channel_id=1, source_target_pairs={{1,0},{2,1},{3,2},{0,3},{5,4},{6,5},{7,6},{4,7},{9,8},{10,9},{11,1... | collective-permute-start | bytes 12296 | tf_op jit(solution)/shard_map/ppermute | solution.py:25
  383.5 15.2 %collective-permute-start.42 = (f32[1,4,256]{2,1,0:T(4,128)S(1)}, f32[1,4,256]{2,1,0:T(4,128)S(1)}, u32[]{:S(2)}, u32[]{:S(2)}) collective-permute-start(f32[1,4,256]{2,1,0:T(4,128)S(1)} %bitcast.1238), channel_id=1, source_target_pairs={{0,1},{1,2},{2,3},{3,0},{4,5},{5,6},{6,7},{7,4},{8,9},{9,10},{10,1... | collective-permute-start | bytes 12296 | tf_op jit(solution)/shard_map/ppermute | solution.py:22
  392.3 7.0 %collective-permute-start.41 = (f32[1,4,3,256]{3,2,1,0:T(4,128)S(1)}, f32[1,4,3,256]{3,2,1,0:T(4,128)S(1)}, u32[]{:S(2)}, u32[]{:S(2)}) collective-permute-start(f32[1,4,3,256]{3,2,1,0:T(4,128)S(1)} %stack_reshape.87), channel_id=1, source_target_pairs={{4,0},{8,4},{12,8},{16,12},{20,16},{24,20},{28,24},{32,28},{36,32}... | collective-permute-start | bytes 36872 | tf_op jit(solution)/shard_map/ppermute | solution.py:25
  395.7 8.4 %collective-permute-start.40 = (f32[1,4,3,256]{3,2,1,0:T(4,128)S(1)}, f32[1,4,3,256]{3,2,1,0:T(4,128)S(1)}, u32[]{:S(2)}, u32[]{:S(2)}) collective-permute-start(f32[1,4,3,256]{3,2,1,0:T(4,128)S(1)} %stack_reshape.86), channel_id=1, source_target_pairs={{0,4},{4,8},{8,12},{12,16},{16,20},{20,24},{24,28},{28,32},{32,36}... | collective-permute-start | bytes 36872 | tf_op jit(solution)/shard_map/ppermute | solution.py:22
  (156 other events, 1056.7 us)
where the time goes:
time: 419 us; the launch traced here: 411 us
  starting transfers between devices  149 us (36%)
  local copies, waits for them, and re-layouts  98 us (23%)
  matrix products  85.2 us (20%)
  waiting for transfers between devices  39.1 us (9%)
  other arithmetic  31.4 us (7%)
  between operations  8.27 us (2%)
    ppermute x22, starting transfers between devices, with_halo(): lax.ppermute(lax.slice_in_dim(block, block.shape[dim] - width, None, axis...  88.7 us
    ppermute x22, starting transfers between devices, with_halo(): lax.ppermute(lax.slice_in_dim(block, 0, width, axis=dim), axis, backward)  60.6 us
    ppermute x22, waiting for transfers between devices, with_halo(): lax.ppermute(lax.slice_in_dim(block, block.shape[dim] - width, None, axis...  39.1 us
    dot_general x66, matrix products, traces(): jnp.einsum('eck,ebk->ebc', interpolate, halfway, precision=precise)  15.7 us
    dot_general x66, matrix products, face_apply(): jnp.einsum('ebj,ebk->ejk', interpolate, halfway, precision=precise)  15.1 us
    dot_general x66, matrix products, traces(): halfway = jnp.einsum('ebj,ejk->ebk', interpolate, face, precision=precise)  15 us
    dot_general x66, matrix products, face_apply(): jnp.einsum('ebc,eck->ebk', jump_term, interpolate, precision=precise)  14.8 us
  transfers between devices with their start and end apart: 44, of which 10 were waited for; matrix products, arithmetic and copies ran while one was open for 37% of the time, Pallas kernels for 0%

commit v1 on v0

v1 whole, which is shorter than its diff:
```python
import functools

import jax
import jax.numpy as jnp
import ml_dtypes
import numpy as np
from jax import lax
from jax.experimental import pallas as pl
from jax.experimental.pallas import tpu as pltpu
from jax.sharding import PartitionSpec as P

MESH = pl.DeviceIdType.MESH
SLOTS = 16
mass_weight = 0.5
penalty = 0.5
cheb_high = 4.0
cheb_low = 0.15


def cheb_nodes(degree):
    return -np.cos(np.pi * np.arange(degree + 1) / degree)


def bary_weights(npoints):
    weights = (-1.0) ** np.arange(npoints)
    weights[0] = 0.5 * weights[0]
    weights[-1] = 0.5 * weights[-1]
    return weights


def lagrange_table(source, target):
    weights = bary_weights(source.shape[0])
    spacing = target[:, None] - source[None, :]
    coincide = np.abs(spacing) < 1e-12
    fractions = weights[None, :] / np.where(coincide, 1.0, spacing)
    lookup = fractions / fractions.sum(axis=1, keepdims=True)
    return np.where(coincide.any(axis=1, keepdims=True), np.where(coincide, 1.0, 0.0), lookup)


def quad_weights(degree):
    weights = np.full(degree + 1, np.pi / degree)
    weights[0] = 0.5 * weights[0]
    weights[-1] = 0.5 * weights[-1]
    return weights


def derivative(degree):
    points = cheb_nodes(degree)
    weights = bary_weights(degree + 1)
    spacing = points[:, None] - points[None, :] + np.eye(degree + 1)
    lookup = weights[None, :] / weights[:, None] / spacing
    lookup = lookup * (1.0 - np.eye(degree + 1))
    return lookup - np.eye(degree + 1) * lookup.sum(axis=1)[:, None]


def level_degree(degree, level_index):
    return [degree, degree // 2, 1][level_index]


def split3(table):
    high = table.astype(ml_dtypes.bfloat16)
    rest = table - high.astype(np.float64)
    middle = rest.astype(ml_dtypes.bfloat16)
    low = (rest - middle.astype(np.float64)).astype(ml_dtypes.bfloat16)
    return high, middle, low


def packed(tables):
    rows = np.concatenate([entry.reshape(9, -1) for entry in tables], axis=1).T
    return np.concatenate(list(split3(rows)) + [np.zeros((rows.shape[0], 5), ml_dtypes.bfloat16)], axis=1)


def order_tables(level_index):
    points = [16, 8, 2][level_index]
    common = cheb_nodes(points - 1)
    common_w = quad_weights(points - 1)
    names = ("scaled", "stiff_diag", "quad_w", "interpolate", "face_diag", "living", "prolong")
    table = {name: [] for name in names}
    for degree in range(7, 16):
        local = level_degree(degree, level_index)
        quad = quad_weights(local)
        deriv = derivative(local)
        stiff = deriv.T @ (quad[:, None] * deriv)
        scaled = np.zeros((points, points))
        scaled[: local + 1, : local + 1] = stiff / quad[:, None]
        padded = lambda vector: np.concatenate([vector, np.zeros(points - local - 1)])
        interp = np.zeros((points, points))
        interp[:, : local + 1] = lagrange_table(cheb_nodes(local), common)
        table["scaled"].append(scaled)
        table["stiff_diag"].append(padded(np.diagonal(stiff)))
        table["quad_w"].append(padded(quad))
        table["interpolate"].append(interp)
        table["face_diag"].append((common_w[:, None] * interp**2).sum(axis=0))
        table["living"].append(padded(np.ones(local + 1)))
        if level_index < 2:
            coarse = level_degree(degree, level_index + 1)
            lift = np.zeros((points, [16, 8, 2][level_index + 1]))
            lift[: local + 1, : coarse + 1] = lagrange_table(cheb_nodes(coarse), cheb_nodes(local))
            table["prolong"].append(lift)
    table = {name: np.stack(table[name]) for name in names if table[name]}
    tau = penalty * (points - 1) ** 2
    table["pair"] = tau * np.outer(common_w, common_w)
    table["tau"] = tau
    return table


def flip(table):
    return np.swapaxes(table, 1, 2)


def constants():
    fine, middle, coarse = [order_tables(level_index) for level_index in range(3)]
    vectors = ("quad_w", "face_diag", "living", "stiff_diag")
    matrices = lambda t: [flip(t["scaled"]), t["scaled"], flip(t["interpolate"]), t["interpolate"]]
    c0 = packed(matrices(fine) + [fine[name] for name in vectors])
    c1 = packed(
        matrices(middle)
        + [middle[name] for name in vectors]
        + [fine["prolong"], flip(fine["prolong"]), flip(middle["prolong"])]
    )
    pairs = [np.repeat(t["pair"], SLOTS, axis=1).astype(np.float32) for t in (fine, middle)]
    return c0, c1, pairs[0], pairs[1], (fine["tau"], middle["tau"]), coarse


def split(values):
    high = values.astype(jnp.bfloat16)
    return high, (values - high.astype(jnp.float32)).astype(jnp.bfloat16)


def dot(left, right):
    return jnp.dot(left, right, preferred_element_type=jnp.float32)


def dot3(values, high, low):
    first, second = split(values)
    return dot(first, high[...]) + dot(second, high[...]) + dot(first, low[...])


def roll(values, shift, axis=-1):
    axis = axis % values.ndim
    return pltpu.roll(values, shift % values.shape[axis], axis)


def lanes_iota(lanes):
    return lax.broadcasted_iota(jnp.int32, (1, lanes), 1)


def rows_iota(rows, lanes):
    return lax.broadcasted_iota(jnp.int32, (rows, lanes), 0)


class Level:
    pass


def resolve(table, place):
    own = lax.broadcasted_iota(jnp.int32, table.shape[1:], 0) == place
    return jnp.sum(jnp.where(own[None], table[...], 0.0), axis=1)


def spread(keep, rows, count, target, low=None):
    keep[: rows.shape[0], : rows.shape[1]] = rows
    lanes = rows.shape[1]
    same = rows_iota(SLOTS, lanes) == (lanes_iota(lanes) & (SLOTS - 1))
    for p in range(count):
        block = jnp.where(same, keep[p : p + 1, :lanes], 0.0)
        high = block.astype(jnp.bfloat16)
        target[p * SLOTS : (p + 1) * SLOTS, :] = high
        if low is not None:
            low[p * SLOTS : (p + 1) * SLOTS, :] = (block - high.astype(jnp.float32)).astype(jnp.bfloat16)


def kernel(taus, coarse, *refs):
    names = iter(refs)
    take = lambda count: [next(names) for _ in range(count)]
    widths_ref, orders_ref, factors_ref, c0_ref, c1_ref, pair0_ref, pair1_ref, res_ref = take(8)
    (out_ref,) = take(1)
    levels = []
    for index in range(2):
        lv = Level()
        lv.n = [16, 8][index]
        lv.lanes = lv.n * SLOTS
        (lv.T, lv.TT, lv.TI, lv.TIT) = take(4)
        (lv.RS, lv.RSl, lv.RI, lv.RIl, lv.RIT, lv.RITl, lv.PP, lv.PPT) = take(8)
        (lv.IL, lv.DINV, lv.WWW, lv.R, lv.X, lv.V, lv.OUT) = take(7)
        (lv.H, lv.Q, lv.G, lv.RZ, lv.U, lv.Y, lv.SB, lv.RB) = take(8)
        lv.pair = [pair0_ref, pair1_ref][index]
        levels.append(lv)
    TP, TPT, PT1, RP, RPl, RPT, RPTl, RP1, RP1l, RPT1, RPT1l, A8, C8, SB2, RB2, KEEP, XIN = take(17)
    send_sem, recv_sem = take(2)

    dom, grp = lax.axis_index("dom"), lax.axis_index("grp")
    n_dom, n_grp = lax.axis_size("dom"), lax.axis_size("grp")
    targets = [
        {"dom": lax.rem(dom + n_dom - 1, n_dom)},
        {"dom": lax.rem(dom + 1, n_dom)},
        {"grp": lax.rem(grp + n_grp - 1, n_grp)},
        {"grp": lax.rem(grp + 1, n_grp)},
    ]
    barrier = pltpu.get_barrier_semaphore()
    for target in targets:
        pl.semaphore_signal(barrier, inc=1, device_id=target, device_id_type=MESH)

    lane = lanes_iota(16 * SLOTS)
    slot = lane & (SLOTS - 1)
    layer = slot & 3
    row = slot >> 2
    width = jnp.int32(0)
    for g in range(4):
        width = jnp.where(grp == g, widths_ref[g], width)
    order = jnp.full(lane.shape, 7, jnp.int32)
    factor = [jnp.full(lane.shape, 1.0, jnp.float32) for _ in range(4)]
    for r in range(4):
        for t in range(3):
            here = slot == r * 4 + t
            order = jnp.where(here, orders_ref[0, r, t], order)
            for c in range(4):
                factor[c] = jnp.where(here, factors_ref[0, r, t, c], factor[c])
    alive = layer < width
    mask = jnp.where(alive, 1.0, 0.0)
    at_first = layer == 0
    at_last = layer == width - 1
    line = rows_iota(32, 16 * SLOTS)
    line = jnp.where(line < 9, line, jnp.where(line < 18, line - 9, jnp.where(line < 27, line - 18, -1)))
    onehot = jnp.where(line == order - 7, 1.0, 0.0).astype(jnp.bfloat16)

    for index, lv in enumerate(levels):
        n, lanes = lv.n, lv.lanes
        lv.place = lane[:, :lanes] >> 4
        lv.last = [order, order >> 1][index][:, :lanes]
        lv.f = [entry[:, :lanes] for entry in factor]
        lv.cm = lv.f[3] * mass_weight
        lv.at_first, lv.at_last = at_first[:, :lanes], at_last[:, :lanes]
        lv.row = row[:, :lanes]
        lv.last_range = [range(7, 16), range(3, 8)][index]
        hot = onehot[:, :lanes]
        source = [c0_ref, c1_ref][index]
        at = 0
        for ref in (lv.T, lv.TT, lv.TI, lv.TIT):
            ref[...] = dot(source[at : at + n * n, :], hot).reshape(n, n, lanes)
            at += n * n
        vectors = dot(source[at : at + 4 * n, :], hot)
        at += 4 * n
        quad, face, live, stiff = [vectors[i * n : (i + 1) * n] for i in range(4)]
        if index == 1:
            TP[...] = dot(source[at : at + 128, :], hot).reshape(16, 8, lanes)
            TPT[...] = dot(source[at + 128 : at + 256, :], hot).reshape(8, 16, lanes)
            PT1[...] = dot(source[at + 256 : at + 272, :], hot).reshape(2, 8, lanes)
        spread(KEEP, resolve(lv.T, lv.place) * lv.f[0], n, lv.RS, lv.RSl)
        inter = resolve(lv.TI, lv.place)
        lv.IL[...] = inter
        spread(KEEP, inter, n, lv.RI, lv.RIl)
        spread(KEEP, resolve(lv.TIT, lv.place), n, lv.RIT, lv.RITl)
        points = rows_iota(n, lanes)
        lv.FM = jnp.where(points == 0, 1.0, 0.0)
        lv.LM = jnp.where(points == lv.last, 1.0, 0.0)
        same = rows_iota(SLOTS, lanes) == (lane[:, :lanes] & (SLOTS - 1))
        one = lambda cond: jnp.where(cond, 1.0, 0.0).astype(jnp.bfloat16)
        for p in range(n):
            rows = slice(p * SLOTS, (p + 1) * SLOTS)
            lv.PP[rows, :lanes] = one(same) if p == 0 else jnp.zeros((SLOTS, lanes), jnp.bfloat16)
            lv.PP[rows, lanes:] = one(same & (lv.last == p))
            lv.PPT[rows, :] = one(same & (lv.place == 0))
            lv.PPT[lanes + p * SLOTS : lanes + (p + 1) * SLOTS, :] = one(same & (lv.place == lv.last))
        pick = lambda table: jnp.sum(jnp.where(points == lv.place, table, 0.0), axis=0, keepdims=True)
        w_i, face_i, live_i, stiff_i = pick(quad), pick(face), pick(live) * mask[:, :lanes], pick(stiff)
        ends = lv.FM + lv.LM
        ends_i = pick(ends)
        f0, f1, f2, _ = lv.f
        for j in range(n):
            one_row = lambda table: table[j : j + 1, :]
            w_j, face_j, live_j, stiff_j, ends_j = [one_row(t) for t in (quad, face, live, stiff, ends)]
            www = (w_i * w_j) * quad
            diagonal = (
                (f0 * stiff_i * w_j) * quad
                + (f1 * w_i * stiff_j) * quad
                + (f2 * w_i * w_j) * stiff
                + lv.cm * www
                + taus[index] * ((ends_j * face_i + face_j * ends_i) * face + (face_j * face_i) * ends)
            )
            node_live = (live_j * live_i) * live
            lv.WWW[j] = www
            lv.DINV[j] = node_live / (diagonal + 1.0 - node_live)
            if index == 0:
                lv.X[j] = node_live
        lv.w_lane = w_i

    fine, middle = levels
    spread(KEEP, resolve(TP, middle.place), 16, RP, RPl)
    wide = jnp.concatenate([TPT[...], TPT[...]], axis=2)
    spread(KEEP, resolve(wide, fine.place), 8, RPT, RPTl)
    place1 = middle.place
    spread(KEEP, jnp.where(place1 == 0, PT1[0], jnp.where(place1 == 1, PT1[1], 0.0)), 8, RP1, RP1l)
    RPT1[...] = jnp.zeros(RPT1.shape, jnp.bfloat16)
    RPT1l[...] = jnp.zeros(RPT1l.shape, jnp.bfloat16)
    spread(KEEP, resolve(PT1, place1), 2, RPT1, RPT1l)

    XIN[...] = jnp.zeros(XIN.shape, jnp.float32)
    for i in range(16):
        for r in range(4):
            XIN[i * SLOTS + r * 4 : i * SLOTS + r * 4 + 3, :] = res_ref[0, r, :, i * 256 : (i + 1) * 256]
    fine.R[...] = jnp.transpose(XIN[...]).reshape(16, 16, 256) * fine.X[...]

    pl.semaphore_wait(barrier, 4)
    pending = []

    def send(number, direction, value, source, landing):
        source[...] = value
        where = number * 4 + direction
        copy = pltpu.make_async_remote_copy(
            src_ref=source,
            dst_ref=landing,
            send_sem=send_sem.at[where],
            recv_sem=recv_sem.at[where],
            device_id=targets[direction],
            device_id_type=MESH,
        )
        copy.start()
        pending.append(copy)
        return copy

    def towards_first(value, last):
        value = jnp.where(last, value, 0.0)
        return value + roll(value, -1) + roll(value, -2)

    def towards_last(value):
        return jnp.where(width == 1, value, jnp.where(width == 2, roll(value, 1), roll(value, 2)))

    def contract(table, source, first, count):
        total = None
        for k in range(table.shape[0]):
            term = table[k][None] * source[first : first + count, k : k + 1, :]
            total = term if total is None else total + term
        return total

    def apply_level(lv, slot_of, number, consume):
        n, lanes = lv.n, lv.lanes
        flat = lv.V[...].reshape(n * n, lanes)
        high, low = split(flat)
        lv.U[...] = (dot(high, lv.PP[...]) + dot(low, lv.PP[...])).reshape(n, n, 2 * lanes)
        y0, z0 = lv.V[0], lv.V[:, 0, :]
        y1, z1 = jnp.zeros_like(y0), jnp.zeros_like(z0)
        for p in lv.last_range:
            here = lv.last == p
            y1 = jnp.where(here, lv.V[p], y1)
            z1 = jnp.where(here, lv.V[:, p, :], z1)
        turned = dot3(jnp.concatenate([z0, z1, y0, y1], axis=0), lv.RI, lv.RIl)
        lv.H[2:6] = turned.reshape(4, n, lanes)
        for f in range(2):
            total = None
            for j in range(n):
                term = lv.IL[j : j + 1, :] * lv.U[j, :, f * lanes : (f + 1) * lanes]
                total = term if total is None else total + term
            lv.H[f] = total
        lv.Q[...] = contract(lv.TI, lv.H, 0, 6)
        outgoing = [lv.Q[0], lv.Q[1], lv.Q[2], towards_first(lv.Q[3], lv.at_last)]
        copies = [
            send(number, d, outgoing[d], lv.SB.at[slot_of, d], lv.RB.at[slot_of, d]) for d in range(4)
        ]
        lv.G[4] = lv.pair[...] * (lv.Q[4] - jnp.where(lv.row > 0, roll(lv.Q[5], 4), 0.0))
        lv.G[5] = lv.pair[...] * (lv.Q[5] - jnp.where(lv.row < 3, roll(lv.Q[4], -4), 0.0))
        back = contract(lv.TIT, lv.G, 4, 2).reshape(2 * n, lanes)
        back = dot3(back, lv.RIT, lv.RITl)
        y_back = [back[:n], back[n:]]
        lv.OUT[...] = (
            dot(high, lv.RS[...]) + dot(low, lv.RS[...]) + dot(high, lv.RSl[...])
        ).reshape(n, n, lanes)
        size = 4 if n == 16 else 8
        for a in range(0, n, size):
            block = slice(a, a + size)
            along_j, along_k = None, None
            for j in range(n):
                term = lv.TT[block, j : j + 1, :] * lv.V[j][None]
                along_j = term if along_j is None else along_j + term
            for k in range(n):
                term = lv.T[k][None] * lv.V[block, k : k + 1, :]
                along_k = term if along_k is None else along_k + term
            lv.OUT[block] = lv.WWW[block] * (
                lv.OUT[block] + lv.f[1] * along_j + lv.f[2] * along_k + lv.cm * lv.V[block]
            )
        lv.OUT[0] = lv.OUT[0] + y_back[0]
        for p in lv.last_range:
            lv.OUT[p] = lv.OUT[p] + jnp.where(lv.last == p, y_back[1], 0.0)
        for copy in copies:
            copy.wait_recv()
        pair = lv.pair[...]
        landed = lambda d: lv.RB[slot_of, d]
        lv.G[0] = pair * (lv.Q[0] - landed(1))
        lv.G[1] = pair * (lv.Q[1] - landed(0))
        lv.G[2] = pair * (lv.Q[2] - jnp.where(lv.at_first, landed(3), roll(lv.Q[3], 1)))
        lv.G[3] = pair * (lv.Q[3] - jnp.where(lv.at_last, towards_last(landed(2)), roll(lv.Q[2], -1)))
        back = contract(lv.TIT, lv.G, 0, 4)
        for f in range(2):
            for j in range(n):
                lv.Y[j, :, f * lanes : (f + 1) * lanes] = lv.IL[j : j + 1, :] * back[f]
        lv.RZ[...] = dot3(back[2:4].reshape(2 * n, lanes), lv.RIT, lv.RITl).reshape(2, n, lanes)
        first, second = split(lv.Y[...].reshape(n * n, 2 * lanes))
        x_back = (dot(first, lv.PPT[...]) + dot(second, lv.PPT[...])).reshape(n, n, lanes)
        for j in range(n):
            z_back = lv.FM * lv.RZ[0, j : j + 1, :] + lv.LM * lv.RZ[1, j : j + 1, :]
            consume(j, lv.OUT[j] + x_back[j] + z_back)

    centre = 0.5 * (cheb_high + cheb_low)
    radius = 0.5 * (cheb_high - cheb_low)
    rho_first = radius / centre
    rho_next = 1.0 / (2.0 * centre / radius - rho_first)
    keep_d = 1.0 + rho_next * rho_first
    take_e = 2.0 * rho_next / radius

    def first_step(lv):
        lv.V[...] = lv.DINV[...] * lv.R[...] * (1.0 / centre)

    def end_pre(lv):
        def consume(j, applied):
            lv.V[j] = keep_d * lv.V[j] + take_e * lv.DINV[j] * (lv.R[j] - applied)

        return consume

    def remainder(lv):
        def consume(j, applied):
            lv.OUT[j] = lv.R[j] - applied

        return consume

    def begin_post(lv):
        def consume(j, applied):
            rest = lv.R[j] - applied
            lv.R[j] = rest
            lv.X[j] = lv.V[j]
            lv.V[j] = lv.DINV[j] * rest * (1.0 / centre)

        return consume

    def end_post(lv):
        def consume(j, applied):
            lv.V[j] = lv.X[j] + keep_d * lv.V[j] + take_e * lv.DINV[j] * (lv.R[j] - applied)

        return consume

    first_step(fine)
    apply_level(fine, 0, 0, end_pre(fine))
    apply_level(fine, 1, 1, remainder(fine))

    lanes_down = dot3(fine.OUT[...].reshape(256, 256), RP, RPl).reshape(16, 16, 128)
    total = None
    for j in range(16):
        term = TPT[:, j : j + 1, :] * lanes_down[j][None]
        total = term if total is None else total + term
    A8[...] = total
    middle.R[...] = contract(TP, A8, 0, 8)
    first_step(middle)
    apply_level(middle, 0, 2, end_pre(middle))
    apply_level(middle, 1, 3, remainder(middle))

    parts = []
    for a in range(2):
        total = None
        for j in range(8):
            term = PT1[a, j : j + 1, :] * middle.OUT[j]
            total = term if total is None else total + term
        for b in range(2):
            parts.append(jnp.sum(PT1[b] * total, axis=0, keepdims=True))
    coarse_r = dot3(jnp.concatenate(parts + [jnp.zeros((4, 128), jnp.float32)], axis=0), RP1, RP1l)

    lane1 = lane[:, :128]
    place2 = lane1 >> 4
    line2 = rows_iota(8, 128)
    low_i = place2 == 0
    low_j = line2 < 2
    low_k = (line2 & 1) == 0
    f0, f1, f2, f3 = middle.f
    s00, s01 = float(coarse["scaled"][0, 0, 0]), float(coarse["scaled"][0, 0, 1])
    w0 = float(coarse["quad_w"][0, 0])
    www = w0**3
    pair2 = float(coarse["pair"][0, 0])
    centre_coeff = www * (s00 * (f0 + f1 + f2) + mass_weight * f3) + 3.0 * pair2
    live2 = jnp.where((place2 < 2) & (line2 < 4), mask[:, :128], 0.0)
    dinv2 = live2 / (centre_coeff + 1.0 - live2)
    inside = live2 > 0.0

    def coarse_apply(v, slot_of, number):
        flip_k = jnp.where(low_k, roll(v, -1, 0), roll(v, 1, 0))
        outgoing = [v, v, flip_k, towards_first(flip_k, middle.at_last)]
        copies = [send(number, d, outgoing[d], SB2.at[slot_of, d], RB2.at[slot_of, d]) for d in range(4)]
        flip_i = jnp.where(low_i, roll(v, -16), roll(v, 16))
        flip_j = jnp.where(low_j, roll(v, -2, 0), roll(v, 2, 0))
        near_y = jnp.where(
            low_j,
            jnp.where(middle.row > 0, roll(flip_j, 4), 0.0),
            jnp.where(middle.row < 3, roll(flip_j, -4), 0.0),
        )
        total = centre_coeff * v + (www * s01) * (f0 * flip_i + f1 * flip_j + f2 * flip_k) - pair2 * near_y
        near_low, near_high = roll(flip_k, 1), roll(flip_k, -1)
        for copy in copies:
            copy.wait_recv()
        landed = lambda d: RB2[slot_of, d]
        near_x = jnp.where(low_i, roll(landed(1), -16), roll(landed(0), 16))
        near_z = jnp.where(
            low_k,
            jnp.where(middle.at_first, landed(3), near_low),
            jnp.where(middle.at_last, towards_last(landed(2)), near_high),
        )
        return jnp.where(inside, total - pair2 * (near_x + near_z), 0.0)

    d = dinv2 * coarse_r * (1.0 / centre)
    x = keep_d * d + take_e * dinv2 * (coarse_r - coarse_apply(d, 0, 4))
    rest = coarse_r - coarse_apply(x, 1, 5)
    d = dinv2 * rest * (1.0 / centre)
    x = x + keep_d * d + take_e * dinv2 * (rest - coarse_apply(d, 2, 6))

    lifted = dot3(x, RPT1, RPT1l)
    columns = []
    for a in range(2):
        columns.append(PT1[0] * lifted[2 * a : 2 * a + 1, :] + PT1[1] * lifted[2 * a + 1 : 2 * a + 2, :])
    for j in range(8):
        middle.V[j] = middle.V[j] + PT1[0, j : j + 1, :] * columns[0] + PT1[1, j : j + 1, :] * columns[1]
    apply_level(middle, 2, 7, begin_post(middle))
    apply_level(middle, 3, 8, end_post(middle))

    C8[...] = contract(TPT, middle.V, 0, 8)
    for j0 in (0, 8):
        total = None
        for a in range(8):
            term = TP[j0 : j0 + 8, a : a + 1, :] * C8[a][None]
            total = term if total is None else total + term
        fine.U[j0 : j0 + 8, :, :128] = total
    lifted = dot3(fine.U[:, :, :128].reshape(256, 128), RPT, RPTl)
    fine.V[...] = fine.V[...] + lifted.reshape(16, 16, 256)
    apply_level(fine, 2, 9, begin_post(fine))
    apply_level(fine, 3, 10, end_post(fine))

    XIN[...] = jnp.transpose(fine.V[...].reshape(256, 256))
    for i in range(16):
        for r in range(4):
            out_ref[0, r, :, i * 256 : (i + 1) * 256] = XIN[i * SLOTS + r * 4 : i * SLOTS + r * 4 + 3, :]
    for copy in pending:
        copy.wait_send()


def scratch():
    f32, b16 = jnp.float32, jnp.bfloat16
    shapes = []
    for n in (16, 8):
        lanes = n * SLOTS
        shapes += [((n, n, lanes), f32)] * 4
        shapes += [((lanes, lanes), b16)] * 6 + [((lanes, 2 * lanes), b16), ((2 * lanes, lanes), b16)]
        shapes += [((n, lanes), f32)] + [((n, n, lanes), f32)] * 6
        shapes += [((6, n, lanes), f32)] * 3 + [((2, n, lanes), f32)]
        shapes += [((n, n, 2 * lanes), f32)] * 2 + [((4, 4, n, lanes), f32)] * 2
    shapes += [((16, 8, 128), f32), ((8, 16, 128), f32), ((2, 8, 128), f32)]
    shapes += [((256, 128), b16)] * 2 + [((128, 256), b16)] * 2 + [((128, 128), b16)] * 4
    shapes += [((8, 16, 128), f32)] * 2 + [((3, 4, 8, 128), f32)] * 2
    shapes += [((16, 256), f32), ((256, 256), f32)]
    semaphores = [pltpu.SemaphoreType.DMA((44,))] * 2
    return [pltpu.VMEM(shape, dtype) for shape, dtype in shapes] + semaphores


def shards(residual, orders, factors, widths):
    c0, c1, pair0, pair1, taus, coarse = constants()
    vmem = pl.BlockSpec(memory_space=pltpu.VMEM)
    smem = pl.BlockSpec(memory_space=pltpu.SMEM)
    return pl.pallas_call(
        functools.partial(kernel, taus, coarse),
        out_shape=jax.ShapeDtypeStruct(residual.shape, jnp.float32),
        in_specs=[smem] * 3 + [vmem] * 5,
        out_specs=vmem,
        scratch_shapes=scratch(),
        compiler_params=pltpu.CompilerParams(
            collective_id=0, has_side_effects=True, vmem_limit_bytes=48 * 1024 * 1024
        ),
    )(widths, orders, factors, jnp.asarray(c0), jnp.asarray(c1), jnp.asarray(pair0), jnp.asarray(pair1), residual)


def solution(mesh):
    return jax.shard_map(
        shards,
        mesh=mesh,
        in_specs=(
            P("dom", None, "grp", None),
            P("dom", None, "grp"),
            P("dom", None, "grp", None),
            P(),
        ),
        out_specs=P("dom", None, "grp", None),
        check_vma=False,
    )
```

time: 419 us -> 73.7 us (0.18); the launches traced: 411 us -> 72.7 us
  starting transfers between devices: 149 us -> 0 us
  local copies, waits for them, and re-layouts: 98 us -> 3.43 us
  matrix products: 85.2 us -> 0 us
  Pallas kernels: 0 us -> 69.2 us
  waiting for transfers between devices: 39.1 us -> 0 us
  other arithmetic: 31.4 us -> 0 us
  between operations: 8.27 us -> 0.06 us
    ppermute x44 -> x0, starting transfers between devices: 149 us -> none  [the longest x22 88.7 us: with_halo(): lax.ppermute(lax.slice_in_dim(block, block.shape[dim] - width, None, axis...]
    dot_general x316 -> x0, matrix products: 81.6 us -> none  [the longest x66 15.7 us: traces(): jnp.einsum('eck,ebk->ebc', interpolate, halfway, precision=precise)]
    pallas_call x0 -> x1, Pallas kernels: none -> 69.2 us  [shards(): pl.pallas_call(functools.partial(kernel, taus, coarse), out_shape=jax.Sha...]
    ppermute x44 -> x0, waiting for transfers between devices: 39.1 us -> none  [the longest x22 39.1 us: with_halo(): lax.ppermute(lax.slice_in_dim(block, block.shape[dim] - width, None, axis...]
    mul x109 -> x0, local copies, waits for them, and re-layouts: 31.9 us -> none  [the longest x9 4.2 us: setup_level(): live_rows[:, None, :] * live_rows[None, :, :] * live_lanes * mask_lanes]
    another operation x83 -> x0, local copies, waits for them, and re-layouts: 14.7 us -> none  [the longest x28 3.96 us: neighbours(): return [entry.reshape(-1, points, points) for entry in nearby]]
    reduce_sum x34 -> x0, other arithmetic: 13.4 us -> none  [the longest x11 6.19 us: volume(): along_x = jnp.sum(stiff_lanes[:, :, None, :] * values[None], axis=1)]
    reshape x101 -> x0, local copies, waits for them, and re-layouts: 11.9 us -> none  [the longest x56 5.13 us: neighbours(): return [entry.reshape(-1, points, points) for entry in nearby]]
  transfers between devices with their start and end apart: 44 -> 0, of which waited for: 10 -> 0; matrix products, arithmetic and copies ran while one was open for 37% -> 0% of each run, Pallas kernels for 0% -> 0%
where the time goes in v1:
time: 73.7 us; the launch traced here: 72.7 us
  Pallas kernels  69.2 us (94%)
  local copies, waits for them, and re-layouts  3.43 us (5%)
    pallas_call x1, Pallas kernels, shards(): pl.pallas_call(functools.partial(kernel, taus, coarse), out_shape=jax.Sha...  69.2 us
    unnamed x13, local copies, waits for them, and re-layouts  2.63 us

profile of v1, /device:TPU:24, one launch (start us, length us, event | category | flops | bytes accessed | tf_op | source)
XLA Modules:
  0.0 72.7 jit_solution(9085751008476134671)
XLA Ops:
  0.0 0.0 copy-start
  0.0 0.8 %copy.9.refs_1_ = s32[1,4,3]{2,1,0:T(4,128)S(1)} copy(s32[1,4,3]{1,0,2:T(1,128)} %param.9) | data formatting | bytes 96 | tf_op args[1]
  0.8 0.7 copy.10.refs_2_
  1.5 0.0 copy-start.1
  1.5 0.0 copy-start.2
  1.5 0.0 copy-start.3
  1.5 0.0 copy-start.4
  1.5 1.1 %copy.11.refs_7_ = f32[1,4,3,4096]{3,2,1,0:T(4,128)S(1)} copy(f32[1,4,3,4096]{3,1,2,0:T(4,128)} %param.8) | data formatting | bytes 393216 | tf_op args[0]
  2.6 0.0 copy-done
  2.6 0.0 copy-done.1
  2.7 0.0 copy-done.2
  2.7 0.0 copy-done.3
  2.7 0.0 copy-done.4
  2.7 69.2 %shard_map.82 = f32[1,4,3,4096]{3,2,1,0:T(4,128)S(1)} custom-call(s32[4]{0:T(128)S(1)} %copy-done.4, s32[1,4,3]{2,1,0:T(4,128)S(1)} %copy.9.refs_1_, f32[1,4,3,4]{3,2,1,0:T(4,128)S(1)} %copy.10.refs_2_, bf16[1088,32]{1,0:T(8,128)(2,1)S(1)} %copy-done, bf16[560,32]{1,0:T(8,128)(2,1)S(1)} %copy-done.1, f32[16,256]{1,0:T(8,128)S(1)} %copy-done.2, ...), custom_call_target="tpu_custom_call" | custom-call | tf_op jit(solution)/shard_map/pallas_call | solution.py:562
  71.9 0.8 %copy.12 = f32[1,4,3,4096]{3,1,2,0:T(4,128)} copy(f32[1,4,3,4096]{3,2,1,0:T(4,128)S(1)} %shard_map.82) | data formatting | bytes 393216 | tf_op jit(solution)/shard_map/pallas_call | solution.py:562
Async XLA Ops:
  0.0 2.6 %copy-start = (bf16[1088,32]{1,0:T(8,128)(2,1)S(1)}, bf16[1088,32]{1,0:T(8,128)(2,1)}, u32[]{:S(2)}) copy-start(bf16[1088,32]{1,0:T(8,128)(2,1)} %constant.8.clone.refs_3_) | copy-start | bytes 208900
  1.5 1.1 %copy-start.1 = (bf16[560,32]{1,0:T(8,128)(2,1)S(1)}, bf16[560,32]{1,0:T(8,128)(2,1)}, u32[]{:S(2)}) copy-start(bf16[560,32]{1,0:T(8,128)(2,1)} %constant.9.clone.refs_4_) | copy-start | bytes 107524
  1.5 1.1 %copy-start.2 = (f32[16,256]{1,0:T(8,128)S(1)}, f32[16,256]{1,0:T(8,128)}, u32[]{:S(2)}) copy-start(f32[16,256]{1,0:T(8,128)} %constant.10.clone.refs_5_) | copy-start | bytes 49156
  1.5 1.2 %copy-start.3 = (f32[8,128]{1,0:T(8,128)S(1)}, f32[8,128]{1,0:T(8,128)}, u32[]{:S(2)}) copy-start(f32[8,128]{1,0:T(8,128)} %constant.11.clone.refs_6_) | copy-start | bytes 12292
  1.5 1.2 %copy-start.4 = (s32[4]{0:T(128)S(1)}, s32[4]{0:T(128)}, u32[]{:S(2)}) copy-start(s32[4]{0:T(128)} %refs_0_.1) | copy-start | bytes 52

commit v2 on v1

--- a/solution.py
+++ b/solution.py
@@ -11,6 +11,14 @@
 
 MESH = pl.DeviceIdType.MESH
 SLOTS = 16
+REACH = 4
+COLUMNS = 2 * REACH + 1
+AROUND = [
+    (dx, dg)
+    for dx in range(-REACH, REACH + 1)
+    for dg in (0, 1, -1, 2)
+    if (dx, dg) != (0, 0) and abs(dg) <= REACH - abs(dx)
+]
 mass_weight = 0.5
 penalty = 0.5
 cheb_high = 4.0
@@ -173,8 +181,9 @@
 def kernel(taus, coarse, *refs):
     names = iter(refs)
     take = lambda count: [next(names) for _ in range(count)]
+    given = take(8)
+    (out_ref,) = take(1)
     widths_ref, orders_ref, factors_ref, c0_ref, c1_ref, pair0_ref, pair1_ref, res_ref = take(8)
-    (out_ref,) = take(1)
     levels = []
     for index in range(2):
         lv = Level()
@@ -187,7 +196,11 @@
         lv.pair = [pair0_ref, pair1_ref][index]
         levels.append(lv)
     TP, TPT, PT1, RP, RPl, RPT, RPTl, RP1, RP1l, RPT1, RPT1l, A8, C8, SB2, RB2, KEEP, XIN = take(17)
-    send_sem, recv_sem = take(2)
+    send_sem, recv_sem, load_sem, wide_send, wide_recv = take(5)
+    landings = [widths_ref, orders_ref, factors_ref, c0_ref, c1_ref, pair0_ref, pair1_ref, res_ref]
+    loads = [pltpu.make_async_copy(*pair, load_sem.at[i]) for i, pair in enumerate(zip(given, landings))]
+    for load in loads:
+        load.start()
 
     dom, grp = lax.axis_index("dom"), lax.axis_index("grp")
     n_dom, n_grp = lax.axis_size("dom"), lax.axis_size("grp")
@@ -198,13 +211,18 @@
         {"grp": lax.rem(grp + 1, n_grp)},
     ]
     barrier = pltpu.get_barrier_semaphore()
-    for target in targets:
+    around = [
+        {"dom": lax.rem(dom + n_dom + dx, n_dom), "grp": lax.rem(grp + n_grp + dg, n_grp)} for dx, dg in AROUND
+    ]
+    for target in around:
         pl.semaphore_signal(barrier, inc=1, device_id=target, device_id_type=MESH)
 
     lane = lanes_iota(16 * SLOTS)
     slot = lane & (SLOTS - 1)
-    layer = slot & 3
-    row = slot >> 2
+    layer = slot >> 2
+    row = slot & 3
+    for load in loads[:3]:
+        load.wait()
     width = jnp.int32(0)
     for g in range(4):
         width = jnp.where(grp == g, widths_ref[g], width)
@@ -212,10 +230,10 @@
     factor = [jnp.full(lane.shape, 1.0, jnp.float32) for _ in range(4)]
     for r in range(4):
         for t in range(3):
-            here = slot == r * 4 + t
-            order = jnp.where(here, orders_ref[0, r, t], order)
+            here = slot == t * 4 + r
+            order = jnp.where(here, orders_ref[t, 0, r], order)
             for c in range(4):
-                factor[c] = jnp.where(here, factors_ref[0, r, t, c], factor[c])
+                factor[c] = jnp.where(here, factors_ref[0, t, r, c], factor[c])
     alive = layer < width
     mask = jnp.where(alive, 1.0, 0.0)
     at_first = layer == 0
@@ -224,7 +242,14 @@
     line = jnp.where(line < 9, line, jnp.where(line < 18, line - 9, jnp.where(line < 27, line - 18, -1)))
     onehot = jnp.where(line == order - 7, 1.0, 0.0).astype(jnp.bfloat16)
 
-    for index, lv in enumerate(levels):
+    def tables(lv, index, which):
+        refs = (lv.TI, lv.TIT, lv.T, lv.TT)
+        source = [c0_ref, c1_ref][index]
+        size = lv.n * lv.n
+        at = (2, 3, 0, 1)[which] * size
+        refs[which][...] = dot(source[at : at + size, :], lv.hot).reshape(lv.n, lv.n, lv.lanes)
+
+    def setup_first(lv, index):
         n, lanes = lv.n, lv.lanes
         lv.place = lane[:, :lanes] >> 4
         lv.last = [order, order >> 1][index][:, :lanes]
@@ -233,35 +258,22 @@
         lv.at_first, lv.at_last = at_first[:, :lanes], at_last[:, :lanes]
         lv.row = row[:, :lanes]
         lv.last_range = [range(7, 16), range(3, 8)][index]
-        hot = onehot[:, :lanes]
-        source = [c0_ref, c1_ref][index]
-        at = 0
-        for ref in (lv.T, lv.TT, lv.TI, lv.TIT):
-            ref[...] = dot(source[at : at + n * n, :], hot).reshape(n, n, lanes)
-            at += n * n
-        vectors = dot(source[at : at + 4 * n, :], hot)
-        at += 4 * n
+        lv.hot = onehot[:, :lanes]
+        tables(lv, index, 0)
+        at = 4 * n * n
+        vectors = dot([c0_ref, c1_ref][index][at : at + 4 * n, :], lv.hot)
         quad, face, live, stiff = [vectors[i * n : (i + 1) * n] for i in range(4)]
-        if index == 1:
-            TP[...] = dot(source[at : at + 128, :], hot).reshape(16, 8, lanes)
-            TPT[...] = dot(source[at + 128 : at + 256, :], hot).reshape(8, 16, lanes)
-            PT1[...] = dot(source[at + 256 : at + 272, :], hot).reshape(2, 8, lanes)
-        spread(KEEP, resolve(lv.T, lv.place) * lv.f[0], n, lv.RS, lv.RSl)
         inter = resolve(lv.TI, lv.place)
         lv.IL[...] = inter
         spread(KEEP, inter, n, lv.RI, lv.RIl)
-        spread(KEEP, resolve(lv.TIT, lv.place), n, lv.RIT, lv.RITl)
         points = rows_iota(n, lanes)
         lv.FM = jnp.where(points == 0, 1.0, 0.0)
         lv.LM = jnp.where(points == lv.last, 1.0, 0.0)
-        same = rows_iota(SLOTS, lanes) == (lane[:, :lanes] & (SLOTS - 1))
-        one = lambda cond: jnp.where(cond, 1.0, 0.0).astype(jnp.bfloat16)
+        lv.same = rows_iota(SLOTS, lanes) == (lane[:, :lanes] & (SLOTS - 1))
         for p in range(n):
             rows = slice(p * SLOTS, (p + 1) * SLOTS)
-            lv.PP[rows, :lanes] = one(same) if p == 0 else jnp.zeros((SLOTS, lanes), jnp.bfloat16)
-            lv.PP[rows, lanes:] = one(same & (lv.last == p))
-            lv.PPT[rows, :] = one(same & (lv.place == 0))
-            lv.PPT[lanes + p * SLOTS : lanes + (p + 1) * SLOTS, :] = one(same & (lv.place == lv.last))
+            lv.PP[rows, :lanes] = one(lv.same) if p == 0 else jnp.zeros((SLOTS, lanes), jnp.bfloat16)
+            lv.PP[rows, lanes:] = one(lv.same & (lv.last == p))
         pick = lambda table: jnp.sum(jnp.where(points == lv.place, table, 0.0), axis=0, keepdims=True)
         w_i, face_i, live_i, stiff_i = pick(quad), pick(face), pick(live) * mask[:, :lanes], pick(stiff)
         ends = lv.FM + lv.LM
@@ -283,26 +295,87 @@
             lv.DINV[j] = node_live / (diagonal + 1.0 - node_live)
             if index == 0:
                 lv.X[j] = node_live
-        lv.w_lane = w_i
-
+
+    def setup_rest(lv, index):
+        n, lanes = lv.n, lv.lanes
+        for which in (1, 2, 3):
+            tables(lv, index, which)
+        spread(KEEP, resolve(lv.T, lv.place) * lv.f[0], n, lv.RS, lv.RSl)
+        spread(KEEP, resolve(lv.TIT, lv.place), n, lv.RIT, lv.RITl)
+        for p in range(n):
+            lv.PPT[p * SLOTS : (p + 1) * SLOTS, :] = one(lv.same & (lv.place == 0))
+            lv.PPT[lanes + p * SLOTS : lanes + (p + 1) * SLOTS, :] = one(lv.same & (lv.place == lv.last))
+
+    def setup_between():
+        at = 4 * 64 + 4 * 8
+        TP[...] = dot(c1_ref[at : at + 128, :], middle.hot).reshape(16, 8, 128)
+        TPT[...] = dot(c1_ref[at + 128 : at + 256, :], middle.hot).reshape(8, 16, 128)
+        PT1[...] = dot(c1_ref[at + 256 : at + 272, :], middle.hot).reshape(2, 8, 128)
+        place1 = middle.place
+        spread(KEEP, resolve(TP, place1), 16, RP, RPl)
+        wide = jnp.concatenate([TPT[...], TPT[...]], axis=2)
+        spread(KEEP, resolve(wide, fine.place), 8, RPT, RPTl)
+        spread(KEEP, jnp.where(place1 == 0, PT1[0], jnp.where(place1 == 1, PT1[1], 0.0)), 8, RP1, RP1l)
+        RPT1[...] = jnp.zeros(RPT1.shape, jnp.bfloat16)
+        RPT1l[...] = jnp.zeros(RPT1l.shape, jnp.bfloat16)
+        spread(KEEP, resolve(PT1, place1), 2, RPT1, RPT1l)
+
+    def setup_middle():
+        setup_first(middle, 1)
+        setup_rest(middle, 1)
+        setup_between()
+
+    one = lambda cond: jnp.where(cond, 1.0, 0.0).astype(jnp.bfloat16)
     fine, middle = levels
-    spread(KEEP, resolve(TP, middle.place), 16, RP, RPl)
-    wide = jnp.concatenate([TPT[...], TPT[...]], axis=2)
-    spread(KEEP, resolve(wide, fine.place), 8, RPT, RPTl)
-    place1 = middle.place
-    spread(KEEP, jnp.where(place1 == 0, PT1[0], jnp.where(place1 == 1, PT1[1], 0.0)), 8, RP1, RP1l)
-    RPT1[...] = jnp.zeros(RPT1.shape, jnp.bfloat16)
-    RPT1l[...] = jnp.zeros(RPT1l.shape, jnp.bfloat16)
-    spread(KEEP, resolve(PT1, place1), 2, RPT1, RPT1l)
-
-    XIN[...] = jnp.zeros(XIN.shape, jnp.float32)
+    for load in loads[3:7]:
+        load.wait()
+    setup_first(fine, 0)
+
+    loads[7].wait()
     for i in range(16):
-        for r in range(4):
-            XIN[i * SLOTS + r * 4 : i * SLOTS + r * 4 + 3, :] = res_ref[0, r, :, i * 256 : (i + 1) * 256]
+        for t in range(3):
+            XIN[i * SLOTS + t * 4 : i * SLOTS + t * 4 + 4, :] = res_ref[0, t, :, i * 256 : (i + 1) * 256]
+        XIN[i * SLOTS + 12 : i * SLOTS + 16, :] = jnp.zeros((4, 256), jnp.float32)
     fine.R[...] = jnp.transpose(XIN[...]).reshape(16, 16, 256) * fine.X[...]
 
-    pl.semaphore_wait(barrier, 4)
+    pl.semaphore_wait(barrier, len(AROUND))
     pending = []
+    lane1 = lane[:, :128]
+    group1 = lane1 >> 5
+
+    def gather_start(which, value):
+        SB2[which] = value
+        for q in range(len(AROUND)):
+            where = which * len(AROUND) + q
+            copy = pltpu.make_async_remote_copy(
+                src_ref=SB2.at[which],
+                dst_ref=RB2.at[which, q],
+                send_sem=wide_send.at[where],
+                recv_sem=wide_recv.at[where],
+                device_id=around[q],
+                device_id_type=MESH,
+            )
+            copy.start()
+            pending.append(copy)
+        return pending[-len(AROUND) :]
+
+    def gather_end(which, value, copies):
+        for copy in copies:
+            copy.wait_recv()
+        columns = []
+        for column in range(-REACH, REACH + 1):
+            total = value if column == 0 else None
+            for q, (dx, _) in enumerate(AROUND):
+                if -dx == column:
+                    total = RB2[which, q] if total is None else total + RB2[which, q]
+            columns.append(total)
+        return jnp.stack(columns)
+
+    own_group = group1 == grp
+    own_factors = jnp.concatenate(
+        [jnp.where(own_group, entry[:, :128], 0.0) for entry in factor] + [jnp.zeros((4, 128), jnp.float32)], axis=0
+    )
+    factor_copies = gather_start(0, own_factors)
 
     def send(number, direction, value, source, landing):
         source[...] = value
@@ -321,10 +394,10 @@
 
     def towards_first(value, last):
         value = jnp.where(last, value, 0.0)
-        return value + roll(value, -1) + roll(value, -2)
+        return value + roll(value, -4) + roll(value, -8)
 
     def towards_last(value):
-        return jnp.where(width == 1, value, jnp.where(width == 2, roll(value, 1), roll(value, 2)))
+        return jnp.where(width == 1, value, jnp.where(width == 2, roll(value, 4), roll(value, 8)))
 
     def contract(table, source, first, count):
         total = None
@@ -333,7 +406,7 @@
             total = term if total is None else total + term
         return total
 
-    def apply_level(lv, slot_of, number, consume):
+    def apply_level(lv, slot_of, number, consume, meanwhile=None, near=None):
         n, lanes = lv.n, lv.lanes
         flat = lv.V[...].reshape(n * n, lanes)
         high, low = split(flat)
@@ -353,12 +426,16 @@
                 total = term if total is None else total + term
             lv.H[f] = total
         lv.Q[...] = contract(lv.TI, lv.H, 0, 6)
-        outgoing = [lv.Q[0], lv.Q[1], lv.Q[2], towards_first(lv.Q[3], lv.at_last)]
-        copies = [
-            send(number, d, outgoing[d], lv.SB.at[slot_of, d], lv.RB.at[slot_of, d]) for d in range(4)
-        ]
-        lv.G[4] = lv.pair[...] * (lv.Q[4] - jnp.where(lv.row > 0, roll(lv.Q[5], 4), 0.0))
-        lv.G[5] = lv.pair[...] * (lv.Q[5] - jnp.where(lv.row < 3, roll(lv.Q[4], -4), 0.0))
+        copies = []
+        if near is None:
+            outgoing = [lv.Q[0], lv.Q[1], lv.Q[2], towards_first(lv.Q[3], lv.at_last)]
+            copies = [
+                send(number, d, outgoing[d], lv.SB.at[slot_of, d], lv.RB.at[slot_of, d]) for d in range(4)
+            ]
+        if meanwhile is not None:
+            meanwhile()
+        lv.G[4] = lv.pair[...] * (lv.Q[4] - jnp.where(lv.row > 0, roll(lv.Q[5], 1), 0.0))
+        lv.G[5] = lv.pair[...] * (lv.Q[5] - jnp.where(lv.row < 3, roll(lv.Q[4], -1), 0.0))
         back = contract(lv.TIT, lv.G, 4, 2).reshape(2 * n, lanes)
         back = dot3(back, lv.RIT, lv.RITl)
         y_back = [back[:n], back[n:]]
@@ -385,10 +462,14 @@
             copy.wait_recv()
         pair = lv.pair[...]
         landed = lambda d: lv.RB[slot_of, d]
-        lv.G[0] = pair * (lv.Q[0] - landed(1))
-        lv.G[1] = pair * (lv.Q[1] - landed(0))
-        lv.G[2] = pair * (lv.Q[2] - jnp.where(lv.at_first, landed(3), roll(lv.Q[3], 1)))
-        lv.G[3] = pair * (lv.Q[3] - jnp.where(lv.at_last, towards_last(landed(2)), roll(lv.Q[2], -1)))
+        if near is None:
+            x_low, x_high, z_low, z_high = landed(1), landed(0), landed(3), towards_last(landed(2))
+        else:
+            x_low, x_high, z_low, z_high = near
+        lv.G[0] = pair * (lv.Q[0] - x_low)
+        lv.G[1] = pair * (lv.Q[1] - x_high)
+        lv.G[2] = pair * (lv.Q[2] - jnp.where(lv.at_first, z_low, roll(lv.Q[3], 4)))
+        lv.G[3] = pair * (lv.Q[3] - jnp.where(lv.at_last, z_high, roll(lv.Q[2], -4)))
         back = contract(lv.TIT, lv.G, 0, 4)
         for f in range(2):
             for j in range(n):
@@ -438,8 +519,8 @@
         return consume
 
     first_step(fine)
-    apply_level(fine, 0, 0, end_pre(fine))
-    apply_level(fine, 1, 1, remainder(fine))
+    apply_level(fine, 0, 0, end_pre(fine), lambda: setup_rest(fine, 0))
+    apply_level(fine, 1, 1, remainder(fine), setup_middle)
 
     lanes_down = dot3(fine.OUT[...].reshape(256, 256), RP, RPl).reshape(16, 16, 128)
     total = None
@@ -462,51 +543,122 @@
             parts.append(jnp.sum(PT1[b] * total, axis=0, keepdims=True))
     coarse_r = dot3(jnp.concatenate(parts + [jnp.zeros((4, 128), jnp.float32)], axis=0), RP1, RP1l)
 
-    lane1 = lane[:, :128]
-    place2 = lane1 >> 4
+    def placed(value):
+        total = value
+        for g in range(1, 4):
+            total = jnp.where(grp == g, roll(value, 32 * g), total)
+        return total
+
+    def unplaced(value):
+        total = value
+        for g in range(1, 4):
+            total = jnp.where(grp == g, roll(value, -32 * g), total)
+        return jnp.where(lane1 < 32, total, 0.0)
+
+    own_r = placed(coarse_r)
+    r_copies = gather_start(1, own_r)
+
+    fs = gather_end(0, own_factors, factor_copies)
+    f0, f1, f2, f3 = [fs[:, c : c + 1, :] for c in range(4)]
     line2 = rows_iota(8, 128)
-    low_i = place2 == 0
+    low_i = ((lane1 >> 4) & 1) == 0
     low_j = line2 < 2
     low_k = (line2 & 1) == 0
-    f0, f1, f2, f3 = middle.f
+    row2, layer2 = lane1 & 3, (lane1 >> 2) & 3
+    width2, before2 = jnp.zeros((1, 128), jnp.int32), jnp.zeros((1, 128), jnp.int32)
+    for g in range(4):
+        width2 = jnp.where(group1 == g, widths_ref[g], width2)
+        before2 = jnp.where(group1 == (g + 1) % 4, widths_ref[g], before2)
     s00, s01 = float(coarse["scaled"][0, 0, 0]), float(coarse["scaled"][0, 0, 1])
     w0 = float(coarse["quad_w"][0, 0])
     www = w0**3
     pair2 = float(coarse["pair"][0, 0])
     centre_coeff = www * (s00 * (f0 + f1 + f2) + mass_weight * f3) + 3.0 * pair2
-    live2 = jnp.where((place2 < 2) & (line2 < 4), mask[:, :128], 0.0)
+    live2 = jnp.where((layer2 < width2) & (line2 < 4), 1.0, 0.0)[None]
     dinv2 = live2 / (centre_coeff + 1.0 - live2)
-    inside = live2 > 0.0
-
-    def coarse_apply(v, slot_of, number):
-        flip_k = jnp.where(low_k, roll(v, -1, 0), roll(v, 1, 0))
-        outgoing = [v, v, flip_k, towards_first(flip_k, middle.at_last)]
-        copies = [send(number, d, outgoing[d], SB2.at[slot_of, d], RB2.at[slot_of, d]) for d in range(4)]
-        flip_i = jnp.where(low_i, roll(v, -16), roll(v, 16))
-        flip_j = jnp.where(low_j, roll(v, -2, 0), roll(v, 2, 0))
+    f0, f1, f2 = [(www * s01) * entry for entry in (f0, f1, f2)]
+
+    def sideways(value, shift):
+        return roll(value.reshape(-1, 128), shift).reshape(value.shape)
+
+    def next_layer(value):
+        across = jnp.where(
+            width2 == 1, sideways(value, -32), jnp.where(width2 == 2, sideways(value, -28), sideways(value, -24))
+        )
+        return jnp.where(layer2 < width2 - 1, sideways(value, -4), across)
+
+    def last_layer(value):
+        across = jnp.where(
+            before2 == 1, sideways(value, 32), jnp.where(before2 == 2, sideways(value, 28), sideways(value, 24))
+        )
+        return jnp.where(layer2 > 0, sideways(value, 4), across)
+
+    def other_k(value):
+        return jnp.where(low_k, roll(value, -1, 1), roll(value, 1, 1))
+
+    def coarse_apply(value, skip):
+        mid = value[1:-1]
+        part = slice(skip, COLUMNS - skip)
+        flip_i = jnp.where(low_i, sideways(mid, -16), sideways(mid, 16))
+        flip_j = jnp.where(low_j, roll(mid, -2, 1), roll(mid, 2, 1))
+        flip_k = other_k(mid)
+        near_x = jnp.where(low_i, sideways(value[:-2], -16), sideways(value[2:], 16))
         near_y = jnp.where(
             low_j,
-            jnp.where(middle.row > 0, roll(flip_j, 4), 0.0),
-            jnp.where(middle.row < 3, roll(flip_j, -4), 0.0),
+            jnp.where(row2 > 0, sideways(flip_j, 1), 0.0),
+            jnp.where(row2 < 3, sideways(flip_j, -1), 0.0),
         )
-        total = centre_coeff * v + (www * s01) * (f0 * flip_i + f1 * flip_j + f2 * flip_k) - pair2 * near_y
-        near_low, near_high = roll(flip_k, 1), roll(flip_k, -1)
-        for copy in copies:
-            copy.wait_recv()
-        landed = lambda d: RB2[slot_of, d]
-        near_x = jnp.where(low_i, roll(landed(1), -16), roll(landed(0), 16))
-        near_z = jnp.where(
-            low_k,
-            jnp.where(middle.at_first, landed(3), near_low),
-            jnp.where(middle.at_last, towards_last(landed(2)), near_high),
+        near_z = jnp.where(low_k, last_layer(flip_k), next_layer(flip_k))
+        return (
+            centre_coeff[part] * mid
+            + (f0[part] * flip_i + f1[part] * flip_j + f2[part] * flip_k)
+            - pair2 * (near_x + near_y + near_z)
         )
-        return jnp.where(inside, total - pair2 * (near_x + near_z), 0.0)
-
-    d = dinv2 * coarse_r * (1.0 / centre)
-    x = keep_d * d + take_e * dinv2 * (coarse_r - coarse_apply(d, 0, 4))
-    rest = coarse_r - coarse_apply(x, 1, 5)
-    d = dinv2 * rest * (1.0 / centre)
-    x = x + keep_d * d + take_e * dinv2 * (rest - coarse_apply(d, 2, 6))
+
+    rs = gather_end(1, own_r, r_copies)
+    d = dinv2 * rs * (1.0 / centre)
+    xs = keep_d * d[1:-1] + take_e * dinv2[1:-1] * (rs[1:-1] - coarse_apply(d, 1))
+    rest = rs[2:-2] - coarse_apply(xs, 2)
+    d = dinv2[2:-2] * rest * (1.0 / centre)
+    xs = xs[2:-2] + keep_d * d[1:-1] + take_e * dinv2[3:-3] * (rest[1:-1] - coarse_apply(d, 3))
+    x = unplaced(xs[1])
+
+    points = cheb_nodes(7)
+    along_lane, along_row = jnp.zeros((1, 128), jnp.float32), jnp.zeros((8, 128), jnp.float32)
+    for b in range(8):
+        along_lane = jnp.where((lane1 >> 4) == b, float(points[b]), along_lane)
+        along_row = jnp.where(line2 == b, float(points[b]), along_row)
+    lane_ends = [0.5 - 0.5 * along_lane, 0.5 + 0.5 * along_lane]
+    row_ends = [0.5 - 0.5 * along_row, 0.5 + 0.5 * along_row]
+
+    def all_lanes(value, end):
+        value = jnp.where(lane1 < 16, roll(value, -16) if end else value, 0.0)
+        value = value + roll(value, 16)
+        value = value + roll(value, 32)
+        return value + roll(value, 64)
+
+    def x_trace(column, end):
+        face = all_lanes(unplaced(column), end)
+        total = 0.0
+        for k in range(2):
+            line = lane_ends[0] * face[k : k + 1, :] + lane_ends[1] * face[2 + k : 3 + k, :]
+            total = total + row_ends[k] * line
+        return total
+
+    def z_trace(column, k):
+        column = unplaced(column)
+        face = lane_ends[0] * all_lanes(column, 0) + lane_ends[1] * all_lanes(column, 1)
+        return row_ends[0] * face[k : k + 1, :] + row_ends[1] * face[2 + k : 3 + k, :]
+
+    turned = other_k(xs[1:2])
+    correction_traces = [
+        x_trace(xs[0], 1),
+        x_trace(xs[2], 0),
+        z_trace(last_layer(turned)[0], 0),
+        z_trace(next_layer(turned)[0], 1),
+    ]
+    before = [middle.RB[1, 1], middle.RB[1, 0], middle.RB[1, 3], towards_last(middle.RB[1, 2])]
+    middle_near = [old + new for old, new in zip(before, correction_traces)]
 
     lifted = dot3(x, RPT1, RPT1l)
     columns = []
@@ -514,7 +666,7 @@
         columns.append(PT1[0] * lifted[2 * a : 2 * a + 1, :] + PT1[1] * lifted[2 * a + 1 : 2 * a + 2, :])
     for j in range(8):
         middle.V[j] = middle.V[j] + PT1[0, j : j + 1, :] * columns[0] + PT1[1, j : j + 1, :] * columns[1]
-    apply_level(middle, 2, 7, begin_post(middle))
+    apply_level(middle, 2, None, begin_post(middle), near=middle_near)
     apply_level(middle, 3, 8, end_post(middle))
 
     C8[...] = contract(TPT, middle.V, 0, 8)
@@ -531,13 +683,13 @@
 
     XIN[...] = jnp.transpose(fine.V[...].reshape(256, 256))
     for i in range(16):
-        for r in range(4):
-            out_ref[0, r, :, i * 256 : (i + 1) * 256] = XIN[i * SLOTS + r * 4 : i * SLOTS + r * 4 + 3, :]
+        for t in range(3):
+            out_ref[0, t, :, i * 256 : (i + 1) * 256] = XIN[i * SLOTS + t * 4 : i * SLOTS + t * 4 + 4, :]
     for copy in pending:
         copy.wait_send()
 
 
-def scratch():
+def scratch(given):
     f32, b16 = jnp.float32, jnp.bfloat16
     shapes = []
     for n in (16, 8):
@@ -549,26 +701,37 @@
         shapes += [((n, n, 2 * lanes), f32)] * 2 + [((4, 4, n, lanes), f32)] * 2
     shapes += [((16, 8, 128), f32), ((8, 16, 128), f32), ((2, 8, 128), f32)]
     shapes += [((256, 128), b16)] * 2 + [((128, 256), b16)] * 2 + [((128, 128), b16)] * 4
-    shapes += [((8, 16, 128), f32)] * 2 + [((3, 4, 8, 128), f32)] * 2
+    shapes += [((8, 16, 128), f32)] * 2 + [((2, 8, 128), f32), ((2, len(AROUND), 8, 128), f32)]
     shapes += [((16, 256), f32), ((256, 256), f32)]
-    semaphores = [pltpu.SemaphoreType.DMA((44,))] * 2
-    return [pltpu.VMEM(shape, dtype) for shape, dtype in shapes] + semaphores
+    semaphores = [pltpu.SemaphoreType.DMA((44,))] * 2 + [pltpu.SemaphoreType.DMA((8,))]
+    semaphores += [pltpu.SemaphoreType.DMA((2 * len(AROUND),))] * 2
+    landings = [pltpu.SMEM(x.shape, x.dtype) for x in given[:3]] + [pltpu.VMEM(x.shape, x.dtype) for x in given[3:]]
+    return landings + [pltpu.VMEM(shape, dtype) for shape, dtype in shapes] + semaphores
 
 
 def shards(residual, orders, factors, widths):
     c0, c1, pair0, pair1, taus, coarse = constants()
-    vmem = pl.BlockSpec(memory_space=pltpu.VMEM)
-    smem = pl.BlockSpec(memory_space=pltpu.SMEM)
-    return pl.pallas_call(
+    given = [
+        widths,
+        jnp.transpose(orders, (2, 0, 1)),
+        jnp.transpose(factors, (0, 2, 1, 3)),
+        jnp.asarray(c0),
+        jnp.asarray(c1),
+        jnp.asarray(pair0),
+        jnp.asarray(pair1),
+        jnp.transpose(residual, (0, 2, 1, 3)),
+    ]
+    out = pl.pallas_call(
         functools.partial(kernel, taus, coarse),
-        out_shape=jax.ShapeDtypeStruct(residual.shape, jnp.float32),
-        in_specs=[smem] * 3 + [vmem] * 5,
-        out_specs=vmem,
-        scratch_shapes=scratch(),
+        out_shape=jax.ShapeDtypeStruct((1, 3, 4, 4096), jnp.float32),
+        in_specs=[pl.BlockSpec(memory_space=pltpu.HBM)] * 8,
+        out_specs=pl.BlockSpec(memory_space=pltpu.VMEM),
+        scratch_shapes=scratch(given),
         compiler_params=pltpu.CompilerParams(
-            collective_id=0, has_side_effects=True, vmem_limit_bytes=48 * 1024 * 1024
+            collective_id=0, has_side_effects=True, vmem_limit_bytes=62 * 1024 * 1024
         ),
-    )(widths, orders, factors, jnp.asarray(c0), jnp.asarray(c1), jnp.asarray(pair0), jnp.asarray(pair1), residual)
+    )(*given)
+    return jnp.transpose(out, (0, 2, 1, 3))
 
 
 def solution(mesh):

time: 73.7 us -> 66.6 us (0.904)
  Pallas kernels: 69.2 us -> 64.7 us
  local copies, waits for them, and re-layouts: 3.43 us -> 1.62 us
    pallas_call x1, Pallas kernels: 69.2 us -> 64.7 us  [shards(): pl.pallas_call(functools.partial(kernel, taus, coarse), out_shape=jax.Sha...]
    unnamed x13 -> x1, local copies, waits for them, and re-layouts: 2.63 us -> 1.62 us
    pallas_call x1 -> x0, local copies, waits for them, and re-layouts: 0.81 us -> none  [shards(): pl.pallas_call(functools.partial(kernel, taus, coarse), out_shape=jax.Sha...]
where the time goes in v2:
time: 66.6 us; the launch traced here: 66.3 us
  Pallas kernels  64.7 us (97%)
  local copies, waits for them, and re-layouts  1.62 us (2%)
    pallas_call x1, Pallas kernels, shards(): pl.pallas_call(functools.partial(kernel, taus, coarse), out_shape=jax.Sha...  64.7 us
    unnamed x1, local copies, waits for them, and re-layouts  1.62 us

profile of v2, /device:TPU:24, one launch (start us, length us, event | category | flops | bytes accessed | tf_op | source)
XLA Modules:
  0.0 66.3 jit_solution(4334815654031939820)
XLA Ops:
  0.0 64.7 %shard_map.82 = f32[1,3,4,4096]{3,2,1,0:T(4,128)} custom-call(s32[4]{0:T(128)} %refs_0_.1, s32[3,1,4]{2,1,0:T(1,128)} %bitcast.7, f32[1,3,4,4]{3,2,1,0:T(4,128)} %bitcast.6, bf16[1088,32]{1,0:T(8,128)(2,1)} %constant.8.clone.refs_3_, bf16[560,32]{1,0:T(8,128)(2,1)} %constant.9.clone.refs_4_, f32[16,256]{1,0:T(8,128)} %constant.10.clone.refs_5_, ...), custom_call_target="tpu_custom_call" | custom-call | tf_op jit(solution)/shard_map/pallas_call | solution.py:724
  64.7 1.6 %copy.10 = f32[1,4,3,4096]{3,1,2,0:T(4,128)} copy(f32[1,4,3,4096]{3,1,2,0:T(4,128)} %bitcast.4) | data formatting | bytes 393216

commit v3 on v2

--- a/solution.py
+++ b/solution.py
@@ -11,7 +11,7 @@
 
 MESH = pl.DeviceIdType.MESH
 SLOTS = 16
-REACH = 4
+REACH = 5
 COLUMNS = 2 * REACH + 1
 AROUND = [
     (dx, dg)
@@ -195,7 +195,7 @@
         (lv.H, lv.Q, lv.G, lv.RZ, lv.U, lv.Y, lv.SB, lv.RB) = take(8)
         lv.pair = [pair0_ref, pair1_ref][index]
         levels.append(lv)
-    TP, TPT, PT1, RP, RPl, RPT, RPTl, RP1, RP1l, RPT1, RPT1l, A8, C8, SB2, RB2, KEEP, XIN = take(17)
+    TP, TPT, PT1, RP, RPl, RPT, RPTl, RP1, RP1l, RPT1, RPT1l, A8, C8, SBF, RBF, SBR, RBR, KEEP, XIN = take(19)
     send_sem, recv_sem, load_sem, wide_send, wide_recv = take(5)
     landings = [widths_ref, orders_ref, factors_ref, c0_ref, c1_ref, pair0_ref, pair1_ref, res_ref]
     loads = [pltpu.make_async_copy(*pair, load_sem.at[i]) for i, pair in enumerate(zip(given, landings))]
@@ -343,31 +343,36 @@
     lane1 = lane[:, :128]
     group1 = lane1 >> 5
 
-    def gather_start(which, value):
-        SB2[which] = value
-        for q in range(len(AROUND)):
+    def gather_start(which, value, reach):
+        source, landing = [(SBF, RBF), (SBR, RBR)][which]
+        source[...] = value
+        copies = {}
+        for q, (dx, dg) in enumerate(AROUND):
+            if abs(dx) + abs(dg) > reach:
+                continue
             where = which * len(AROUND) + q
-            copy = pltpu.make_async_remote_copy(
-                src_ref=SB2.at[which],
-                dst_ref=RB2.at[which, q],
+            copies[q] = pltpu.make_async_remote_copy(
+                src_ref=source,
+                dst_ref=landing.at[q],
                 send_sem=wide_send.at[where],
                 recv_sem=wide_recv.at[where],
                 device_id=around[q],
                 device_id_type=MESH,
             )
-            copy.start()
-            pending.append(copy)
-        return pending[-len(AROUND) :]
-
-    def gather_end(which, value, copies):
-        for copy in copies:
-            copy.wait_recv()
+            copies[q].start()
+            pending.append(copies[q])
+        return copies
+
+    def gather_end(which, value, reach, copies):
+        landing = [RBF, RBR][which]
+        for q in copies:
+            copies[q].wait_recv()
         columns = []
-        for column in range(-REACH, REACH + 1):
+        for column in range(-reach, reach + 1):
             total = value if column == 0 else None
-            for q, (dx, _) in enumerate(AROUND):
-                if -dx == column:
-                    total = RB2[which, q] if total is None else total + RB2[which, q]
+            for q in copies:
+                if -AROUND[q][0] == column:
+                    total = landing[q] if total is None else total + landing[q]
             columns.append(total)
         return jnp.stack(columns)
 
@@ -375,7 +380,7 @@
     own_factors = jnp.concatenate(
         [jnp.where(own_group, entry[:, :128], 0.0) for entry in factor] + [jnp.zeros((4, 128), jnp.float32)], axis=0
     )
-    factor_copies = gather_start(0, own_factors)
+    factor_copies = gather_start(0, own_factors, REACH - 1)
 
     def send(number, direction, value, source, landing):
         source[...] = value
@@ -406,7 +411,7 @@
             total = term if total is None else total + term
         return total
 
-    def apply_level(lv, slot_of, number, consume, meanwhile=None, near=None):
+    def apply_level(lv, slot_of, number, consume, meanwhile=None, near=None, defer=False):
         n, lanes = lv.n, lv.lanes
         flat = lv.V[...].reshape(n * n, lanes)
         high, low = split(flat)
@@ -458,8 +463,11 @@
         lv.OUT[0] = lv.OUT[0] + y_back[0]
         for p in lv.last_range:
             lv.OUT[p] = lv.OUT[p] + jnp.where(lv.last == p, y_back[1], 0.0)
-        for copy in copies:
-            copy.wait_recv()
+        if defer:
+            lv.deferred, near = copies, [0.0] * 4
+        else:
+            for copy in copies:
+                copy.wait_recv()
         pair = lv.pair[...]
         landed = lambda d: lv.RB[slot_of, d]
         if near is None:
@@ -531,7 +539,7 @@
     middle.R[...] = contract(TP, A8, 0, 8)
     first_step(middle)
     apply_level(middle, 0, 2, end_pre(middle))
-    apply_level(middle, 1, 3, remainder(middle))
+    apply_level(middle, 1, 3, remainder(middle), defer=True)
 
     parts = []
     for a in range(2):
@@ -555,12 +563,39 @@
             total = jnp.where(grp == g, roll(value, -32 * g), total)
         return jnp.where(lane1 < 32, total, 0.0)
 
-    own_r = placed(coarse_r)
-    r_copies = gather_start(1, own_r)
-
-    fs = gather_end(0, own_factors, factor_copies)
+    points = cheb_nodes(7)
+    line2 = rows_iota(8, 128)
+    along_lane, along_row = jnp.zeros((1, 128), jnp.float32), jnp.zeros((8, 128), jnp.float32)
+    for b in range(8):
+        along_lane = jnp.where((lane1 >> 4) == b, float(points[b]), along_lane)
+        along_row = jnp.where(line2 == b, float(points[b]), along_row)
+    lane_ends = [0.5 - 0.5 * along_lane, 0.5 + 0.5 * along_lane]
+    row_ends = [0.5 - 0.5 * along_row, 0.5 + 0.5 * along_row]
+
+    def row_sums(face):
+        weighted = middle.pair[...] * middle.Q[face]
+        return [jnp.sum(row_ends[end] * weighted, axis=0, keepdims=True) for end in range(2)]
+
+    def group_sums(rows):
+        total = jnp.concatenate(rows, axis=0)
+        for shift in (16, 32, 64):
+            total = total + roll(total, shift)
+        return total
+
+    def two_groups(low, high):
+        return jnp.where(lane1 < 16, low, jnp.where(lane1 < 32, high, 0.0))
+
+    x_rows = [lane_ends[j] * row_sums(f)[k] for f in range(2) for j in range(2) for k in range(2)]
+    x_sums = group_sums(x_rows)
+    z_rows = [lane_ends[i] * row_sums(2 + k)[j] for i in range(2) for j in range(2) for k in range(2)]
+    z_sums = group_sums(z_rows)
+    x_given = two_groups(x_sums[:4], x_sums[4:])
+    z_given = two_groups(z_sums[:4], z_sums[4:])
+    own_r = placed(jnp.concatenate([coarse_r[:4], x_given, z_given, jnp.zeros((4, 128), jnp.float32)], axis=0))
+    r_copies = gather_start(1, own_r, REACH)
+
+    fs = gather_end(0, own_factors, REACH - 1, factor_copies)
     f0, f1, f2, f3 = [fs[:, c : c + 1, :] for c in range(4)]
-    line2 = rows_iota(8, 128)
     low_i = ((lane1 >> 4) & 1) == 0
     low_j = line2 < 2
     low_k = (line2 & 1) == 0
@@ -598,7 +633,7 @@
 
     def coarse_apply(value, skip):
         mid = value[1:-1]
-        part = slice(skip, COLUMNS - skip)
+        part = slice(skip, COLUMNS - 2 - skip)
         flip_i = jnp.where(low_i, sideways(mid, -16), sideways(mid, 16))
         flip_j = jnp.where(low_j, roll(mid, -2, 1), roll(mid, 2, 1))
         flip_k = other_k(mid)
@@ -615,21 +650,22 @@
             - pair2 * (near_x + near_y + near_z)
         )
 
-    rs = gather_end(1, own_r, r_copies)
+    both = gather_end(1, own_r, REACH, r_copies)
+    upper, lower = both[:, :8], both[:, 8:]
+    given = roll(upper, 4, 1)
+    rs = upper[1:-1] + jnp.where(low_i, sideways(given[:-2], -16), sideways(given[2:], 16))
+    given = other_k(lower[1:-1])
+    rs = rs + jnp.where(
+        low_k,
+        jnp.where(layer2 == 0, last_layer(given), 0.0),
+        jnp.where(layer2 == width2 - 1, next_layer(given), 0.0),
+    )
     d = dinv2 * rs * (1.0 / centre)
     xs = keep_d * d[1:-1] + take_e * dinv2[1:-1] * (rs[1:-1] - coarse_apply(d, 1))
     rest = rs[2:-2] - coarse_apply(xs, 2)
     d = dinv2[2:-2] * rest * (1.0 / centre)
     xs = xs[2:-2] + keep_d * d[1:-1] + take_e * dinv2[3:-3] * (rest[1:-1] - coarse_apply(d, 3))
     x = unplaced(xs[1])
-
-    points = cheb_nodes(7)
-    along_lane, along_row = jnp.zeros((1, 128), jnp.float32), jnp.zeros((8, 128), jnp.float32)
-    for b in range(8):
-        along_lane = jnp.where((lane1 >> 4) == b, float(points[b]), along_lane)
-        along_row = jnp.where(line2 == b, float(points[b]), along_row)
-    lane_ends = [0.5 - 0.5 * along_lane, 0.5 + 0.5 * along_lane]
-    row_ends = [0.5 - 0.5 * along_row, 0.5 + 0.5 * along_row]
 
     def all_lanes(value, end):
         value = jnp.where(lane1 < 16, roll(value, -16) if end else value, 0.0)
@@ -657,6 +693,8 @@
         z_trace(last_layer(turned)[0], 0),
         z_trace(next_layer(turned)[0], 1),
     ]
+    for copy in middle.deferred:
+        copy.wait_recv()
     before = [middle.RB[1, 1], middle.RB[1, 0], middle.RB[1, 3], towards_last(middle.RB[1, 2])]
     middle_near = [old + new for old, new in zip(before, correction_traces)]
 
@@ -701,7 +739,8 @@
         shapes += [((n, n, 2 * lanes), f32)] * 2 + [((4, 4, n, lanes), f32)] * 2
     shapes += [((16, 8, 128), f32), ((8, 16, 128), f32), ((2, 8, 128), f32)]
     shapes += [((256, 128), b16)] * 2 + [((128, 256), b16)] * 2 + [((128, 128), b16)] * 4
-    shapes += [((8, 16, 128), f32)] * 2 + [((2, 8, 128), f32), ((2, len(AROUND), 8, 128), f32)]
+    shapes += [((8, 16, 128), f32)] * 2 + [((8, 128), f32), ((len(AROUND), 8, 128), f32)]
+    shapes += [((16, 128), f32), ((len(AROUND), 16, 128), f32)]
     shapes += [((16, 256), f32), ((256, 256), f32)]
     semaphores = [pltpu.SemaphoreType.DMA((44,))] * 2 + [pltpu.SemaphoreType.DMA((8,))]
     semaphores += [pltpu.SemaphoreType.DMA((2 * len(AROUND),))] * 2

time: 66.6 us -> 64.6 us (0.970)
  Pallas kernels: 64.7 us -> 62 us
    pallas_call x1, Pallas kernels: 64.7 us -> 62 us  [shards(): pl.pallas_call(functools.partial(kernel, taus, coarse), out_shape=jax.Sha...]
where the time goes in v3:
time: 64.6 us; the launch traced here: 63.6 us
  Pallas kernels  62 us (96%)
  local copies, waits for them, and re-layouts  1.62 us (3%)
    pallas_call x1, Pallas kernels, shards(): pl.pallas_call(functools.partial(kernel, taus, coarse), out_shape=jax.Sha...  62 us
    unnamed x1, local copies, waits for them, and re-layouts  1.62 us

profile of v3, /device:TPU:24, one launch (start us, length us, event | category | flops | bytes accessed | tf_op | source)
XLA Modules:
  0.0 63.6 jit_solution(14794130937380484652)
XLA Ops:
  0.0 62.0 %shard_map.82 = f32[1,3,4,4096]{3,2,1,0:T(4,128)} custom-call(s32[4]{0:T(128)} %refs_0_.1, s32[3,1,4]{2,1,0:T(1,128)} %bitcast.7, f32[1,3,4,4]{3,2,1,0:T(4,128)} %bitcast.6, bf16[1088,32]{1,0:T(8,128)(2,1)} %constant.8.clone.refs_3_, bf16[560,32]{1,0:T(8,128)(2,1)} %constant.9.clone.refs_4_, f32[16,256]{1,0:T(8,128)} %constant.10.clone.refs_5_, ...), custom_call_target="tpu_custom_call" | custom-call | tf_op jit(solution)/shard_map/pallas_call | solution.py:763
  62.0 1.6 %copy.10 = f32[1,4,3,4096]{3,1,2,0:T(4,128)} copy(f32[1,4,3,4096]{3,1,2,0:T(4,128)} %bitcast.4) | data formatting | bytes 393216

commit v4 on v3

--- a/solution.py
+++ b/solution.py
@@ -13,12 +13,15 @@
 SLOTS = 16
 REACH = 5
 COLUMNS = 2 * REACH + 1
-AROUND = [
-    (dx, dg)
-    for dx in range(-REACH, REACH + 1)
-    for dg in (0, 1, -1, 2)
-    if (dx, dg) != (0, 0) and abs(dg) <= REACH - abs(dx)
-]
+AROUND = sorted(
+    [
+        (dx, dg)
+        for dx in range(-REACH, REACH + 1)
+        for dg in (0, 1, -1, 2)
+        if (dx, dg) != (0, 0) and abs(dg) <= REACH - abs(dx)
+    ],
+    key=lambda place: -(abs(place[0]) + 3 * abs(place[1])),
+)
 mass_weight = 0.5
 penalty = 0.5
 cheb_high = 4.0
@@ -127,7 +130,14 @@
         + [fine["prolong"], flip(fine["prolong"]), flip(middle["prolong"])]
     )
     pairs = [np.repeat(t["pair"], SLOTS, axis=1).astype(np.float32) for t in (fine, middle)]
-    return c0, c1, pairs[0], pairs[1], (fine["tau"], middle["tau"]), coarse
+    lift = lagrange_table(cheb_nodes(7), cheb_nodes(15))
+    wide = np.kron(lift, np.eye(SLOTS))
+    blank = lambda table, rows, cols: np.pad(table, ((0, rows - table.shape[0]), (0, cols - table.shape[1])))
+    lifts = []
+    for table in (blank(lift, 16, 16), blank(lift.T, 16, 16), wide, wide.T):
+        high = table.astype(ml_dtypes.bfloat16)
+        lifts += [high, (table - high.astype(np.float64)).astype(ml_dtypes.bfloat16)]
+    return lifts, c0, c1, pairs[0], pairs[1], (fine["tau"], middle["tau"]), coarse
 
 
 def split(values):
@@ -181,9 +191,10 @@
 def kernel(taus, coarse, *refs):
     names = iter(refs)
     take = lambda count: [next(names) for _ in range(count)]
-    given = take(8)
+    given = take(16)
     (out_ref,) = take(1)
     widths_ref, orders_ref, factors_ref, c0_ref, c1_ref, pair0_ref, pair1_ref, res_ref = take(8)
+    lift_refs = take(8)
     levels = []
     for index in range(2):
         lv = Level()
@@ -197,7 +208,7 @@
         levels.append(lv)
     TP, TPT, PT1, RP, RPl, RPT, RPTl, RP1, RP1l, RPT1, RPT1l, A8, C8, SBF, RBF, SBR, RBR, KEEP, XIN = take(19)
     send_sem, recv_sem, load_sem, wide_send, wide_recv = take(5)
-    landings = [widths_ref, orders_ref, factors_ref, c0_ref, c1_ref, pair0_ref, pair1_ref, res_ref]
+    landings = [widths_ref, orders_ref, factors_ref, c0_ref, c1_ref, pair0_ref, pair1_ref, res_ref] + lift_refs
     loads = [pltpu.make_async_copy(*pair, load_sem.at[i]) for i, pair in enumerate(zip(given, landings))]
     for load in loads:
         load.start()
@@ -380,7 +391,7 @@
     own_factors = jnp.concatenate(
         [jnp.where(own_group, entry[:, :128], 0.0) for entry in factor] + [jnp.zeros((4, 128), jnp.float32)], axis=0
     )
-    factor_copies = gather_start(0, own_factors, REACH - 1)
+    factor_copies = {}
 
     def send(number, direction, value, source, landing):
         source[...] = value
@@ -411,7 +422,18 @@
             total = term if total is None else total + term
         return total
 
-    def apply_level(lv, slot_of, number, consume, meanwhile=None, near=None, defer=False):
+    def give_back(lv):
+        n, lanes = lv.n, lv.lanes
+        back = contract(lv.TIT, lv.G, 0, 4)
+        for f in range(2):
+            for j in range(n):
+                lv.Y[j, :, f * lanes : (f + 1) * lanes] = lv.IL[j : j + 1, :] * back[f]
+        lv.RZ[...] = dot3(back[2:4].reshape(2 * n, lanes), lv.RIT, lv.RITl).reshape(2, n, lanes)
+        first, second = split(lv.Y[...].reshape(n * n, 2 * lanes))
+        x_back = (dot(first, lv.PPT[...]) + dot(second, lv.PPT[...])).reshape(n, n, lanes)
+        return x_back, lambda j: lv.FM * lv.RZ[0, j : j + 1, :] + lv.LM * lv.RZ[1, j : j + 1, :]
+
+    def apply_level(lv, slot_of, number, consume, meanwhile=None, near=None, defer=False, lead=False):
         n, lanes = lv.n, lv.lanes
         flat = lv.V[...].reshape(n * n, lanes)
         high, low = split(flat)
@@ -437,6 +459,8 @@
             copies = [
                 send(number, d, outgoing[d], lv.SB.at[slot_of, d], lv.RB.at[slot_of, d]) for d in range(4)
             ]
+        if lead:
+            return copies
         if meanwhile is not None:
             meanwhile()
         lv.G[4] = lv.pair[...] * (lv.Q[4] - jnp.where(lv.row > 0, roll(lv.Q[5], 1), 0.0))
@@ -473,21 +497,14 @@
         if near is None:
             x_low, x_high, z_low, z_high = landed(1), landed(0), landed(3), towards_last(landed(2))
         else:
-            x_low, x_high, z_low, z_high = near
+            x_low, x_high, z_low, z_high = near() if callable(near) else near
         lv.G[0] = pair * (lv.Q[0] - x_low)
         lv.G[1] = pair * (lv.Q[1] - x_high)
         lv.G[2] = pair * (lv.Q[2] - jnp.where(lv.at_first, z_low, roll(lv.Q[3], 4)))
         lv.G[3] = pair * (lv.Q[3] - jnp.where(lv.at_last, z_high, roll(lv.Q[2], -4)))
-        back = contract(lv.TIT, lv.G, 0, 4)
-        for f in range(2):
-            for j in range(n):
-                lv.Y[j, :, f * lanes : (f + 1) * lanes] = lv.IL[j : j + 1, :] * back[f]
-        lv.RZ[...] = dot3(back[2:4].reshape(2 * n, lanes), lv.RIT, lv.RITl).reshape(2, n, lanes)
-        first, second = split(lv.Y[...].reshape(n * n, 2 * lanes))
-        x_back = (dot(first, lv.PPT[...]) + dot(second, lv.PPT[...])).reshape(n, n, lanes)
+        x_back, z_back = give_back(lv)
         for j in range(n):
-            z_back = lv.FM * lv.RZ[0, j : j + 1, :] + lv.LM * lv.RZ[1, j : j + 1, :]
-            consume(j, lv.OUT[j] + x_back[j] + z_back)
+            consume(j, lv.OUT[j] + x_back[j] + z_back(j))
 
     centre = 0.5 * (cheb_high + cheb_low)
     radius = 0.5 * (cheb_high - cheb_low)
@@ -526,9 +543,15 @@
 
         return consume
 
+    def after_first_send():
+        for load in loads[8:]:
+            load.wait()
+        factor_copies.update(gather_start(0, own_factors, REACH - 1))
+        setup_rest(fine, 0)
+
     first_step(fine)
-    apply_level(fine, 0, 0, end_pre(fine), lambda: setup_rest(fine, 0))
-    apply_level(fine, 1, 1, remainder(fine), setup_middle)
+    apply_level(fine, 0, 0, end_pre(fine), after_first_send)
+    apply_level(fine, 1, 1, remainder(fine), setup_middle, defer=True)
 
     lanes_down = dot3(fine.OUT[...].reshape(256, 256), RP, RPl).reshape(16, 16, 128)
     total = None
@@ -537,6 +560,22 @@
         total = term if total is None else total + term
     A8[...] = total
     middle.R[...] = contract(TP, A8, 0, 8)
+
+    def on_rows(high, low, values):
+        first, second = split(values)
+        return dot(high[...], first) + dot(high[...], second) + dot(low[...], first)
+
+    for copy in fine.deferred:
+        copy.wait_recv()
+    z_low = jnp.where(fine.at_first, fine.RB[1, 3], 0.0)
+    z_high = jnp.where(fine.at_last, towards_last(fine.RB[1, 2]), 0.0)
+    near_faces = [fine.pair[...] * value for value in (fine.RB[1, 1], fine.RB[1, 0], z_low, z_high)]
+    near_faces = on_rows(lift_refs[2], lift_refs[3], jnp.concatenate(near_faces, axis=1))[:8]
+    near_faces = jnp.concatenate([near_faces[:, f * 256 : (f + 1) * 256] for f in range(4)], axis=0)
+    middle.G[0:4] = dot3(near_faces, lift_refs[4], lift_refs[5]).reshape(4, 8, 128)
+    x_back, z_back = give_back(middle)
+    for j in range(8):
+        middle.R[j] = middle.R[j] + x_back[j] + z_back(j)
     first_step(middle)
     apply_level(middle, 0, 2, end_pre(middle))
     apply_level(middle, 1, 3, remainder(middle), defer=True)
@@ -707,6 +746,8 @@
     apply_level(middle, 2, None, begin_post(middle), near=middle_near)
     apply_level(middle, 3, 8, end_post(middle))
 
+    lead = apply_level(middle, 4, 7, None, lead=True)
+
     C8[...] = contract(TPT, middle.V, 0, 8)
     for j0 in (0, 8):
         total = None
@@ -716,7 +757,18 @@
         fine.U[j0 : j0 + 8, :, :128] = total
     lifted = dot3(fine.U[:, :, :128].reshape(256, 128), RPT, RPTl)
     fine.V[...] = fine.V[...] + lifted.reshape(16, 16, 256)
-    apply_level(fine, 2, 9, begin_post(fine))
+
+    def fine_near():
+        for copy in lead:
+            copy.wait_recv()
+        faces = [middle.RB[4, 1], middle.RB[4, 0], middle.RB[4, 3], towards_last(middle.RB[4, 2])]
+        wide = dot3(jnp.concatenate(faces, axis=0), lift_refs[6], lift_refs[7])
+        wide = jnp.concatenate([wide[f * 8 : (f + 1) * 8] for f in range(4)], axis=1)
+        wide = on_rows(lift_refs[0], lift_refs[1], jnp.concatenate([wide, jnp.zeros_like(wide)], axis=0))
+        before = [fine.RB[1, 1], fine.RB[1, 0], fine.RB[1, 3], towards_last(fine.RB[1, 2])]
+        return [old + wide[:, f * 256 : (f + 1) * 256] for f, old in enumerate(before)]
+
+    apply_level(fine, 2, None, begin_post(fine), near=fine_near)
     apply_level(fine, 3, 10, end_post(fine))
 
     XIN[...] = jnp.transpose(fine.V[...].reshape(256, 256))
@@ -736,20 +788,20 @@
         shapes += [((lanes, lanes), b16)] * 6 + [((lanes, 2 * lanes), b16), ((2 * lanes, lanes), b16)]
         shapes += [((n, lanes), f32)] + [((n, n, lanes), f32)] * 6
         shapes += [((6, n, lanes), f32)] * 3 + [((2, n, lanes), f32)]
-        shapes += [((n, n, 2 * lanes), f32)] * 2 + [((4, 4, n, lanes), f32)] * 2
+        shapes += [((n, n, 2 * lanes), f32)] * 2 + [((5, 4, n, lanes), f32)] * 2
     shapes += [((16, 8, 128), f32), ((8, 16, 128), f32), ((2, 8, 128), f32)]
     shapes += [((256, 128), b16)] * 2 + [((128, 256), b16)] * 2 + [((128, 128), b16)] * 4
     shapes += [((8, 16, 128), f32)] * 2 + [((8, 128), f32), ((len(AROUND), 8, 128), f32)]
     shapes += [((16, 128), f32), ((len(AROUND), 16, 128), f32)]
     shapes += [((16, 256), f32), ((256, 256), f32)]
-    semaphores = [pltpu.SemaphoreType.DMA((44,))] * 2 + [pltpu.SemaphoreType.DMA((8,))]
+    semaphores = [pltpu.SemaphoreType.DMA((44,))] * 2 + [pltpu.SemaphoreType.DMA((16,))]
     semaphores += [pltpu.SemaphoreType.DMA((2 * len(AROUND),))] * 2
     landings = [pltpu.SMEM(x.shape, x.dtype) for x in given[:3]] + [pltpu.VMEM(x.shape, x.dtype) for x in given[3:]]
     return landings + [pltpu.VMEM(shape, dtype) for shape, dtype in shapes] + semaphores
 
 
 def shards(residual, orders, factors, widths):
-    c0, c1, pair0, pair1, taus, coarse = constants()
+    lifts, c0, c1, pair0, pair1, taus, coarse = constants()
     given = [
         widths,
         jnp.transpose(orders, (2, 0, 1)),
@@ -759,11 +811,11 @@
         jnp.asarray(pair0),
         jnp.asarray(pair1),
         jnp.transpose(residual, (0, 2, 1, 3)),
-    ]
+    ] + [jnp.asarray(table) for table in lifts]
     out = pl.pallas_call(
         functools.partial(kernel, taus, coarse),
         out_shape=jax.ShapeDtypeStruct((1, 3, 4, 4096), jnp.float32),
-        in_specs=[pl.BlockSpec(memory_space=pltpu.HBM)] * 8,
+        in_specs=[pl.BlockSpec(memory_space=pltpu.HBM)] * 16,
         out_specs=pl.BlockSpec(memory_space=pltpu.VMEM),
         scratch_shapes=scratch(given),
         compiler_params=pltpu.CompilerParams(

time: 64.6 us -> 62.8 us (0.972)
  Pallas kernels: 62 us -> 60.5 us
    pallas_call x1, Pallas kernels: 62 us -> 60.5 us  [shards(): pl.pallas_call(functools.partial(kernel, taus, coarse), out_shape=jax.Sha...]
where the time goes in v4:
time: 62.8 us; the launch traced here: 62.2 us
  Pallas kernels  60.5 us (96%)
  local copies, waits for them, and re-layouts  1.62 us (3%)
    pallas_call x1, Pallas kernels, shards(): pl.pallas_call(functools.partial(kernel, taus, coarse), out_shape=jax.Sha...  60.5 us
    unnamed x1, local copies, waits for them, and re-layouts  1.62 us

profile of v4, /device:TPU:24, one launch (start us, length us, event | category | flops | bytes accessed | tf_op | source)
XLA Modules:
  0.0 62.2 jit_solution(11686265898722783904)
XLA Ops:
  0.0 60.5 %shard_map.154 = f32[1,3,4,4096]{3,2,1,0:T(4,128)} custom-call(s32[4]{0:T(128)} %refs_0_.1, s32[3,1,4]{2,1,0:T(1,128)} %bitcast.7, f32[1,3,4,4]{3,2,1,0:T(4,128)} %bitcast.6, bf16[1088,32]{1,0:T(8,128)(2,1)} %constant.24.clone.refs_3_, bf16[560,32]{1,0:T(8,128)(2,1)} %constant.25.clone.refs_4_, f32[16,256]{1,0:T(8,128)} %constant.26.clone.refs_5_, ...), custom_call_target="tpu_custom_call" | custom-call | tf_op jit(solution)/shard_map/pallas_call | solution.py:815
  60.6 1.6 %copy.18 = f32[1,4,3,4096]{3,1,2,0:T(4,128)} copy(f32[1,4,3,4096]{3,1,2,0:T(4,128)} %bitcast.4) | data formatting | bytes 393216

commit v5 on v4

--- a/solution.py
+++ b/solution.py
@@ -307,23 +307,29 @@
             if index == 0:
                 lv.X[j] = node_live
 
-    def setup_rest(lv, index):
+    def setup_return(lv, index):
         n, lanes = lv.n, lv.lanes
-        for which in (1, 2, 3):
-            tables(lv, index, which)
-        spread(KEEP, resolve(lv.T, lv.place) * lv.f[0], n, lv.RS, lv.RSl)
+        tables(lv, index, 1)
         spread(KEEP, resolve(lv.TIT, lv.place), n, lv.RIT, lv.RITl)
         for p in range(n):
             lv.PPT[p * SLOTS : (p + 1) * SLOTS, :] = one(lv.same & (lv.place == 0))
             lv.PPT[lanes + p * SLOTS : lanes + (p + 1) * SLOTS, :] = one(lv.same & (lv.place == lv.last))
 
+    def setup_volume(lv, index):
+        tables(lv, index, 2)
+        tables(lv, index, 3)
+        spread(KEEP, resolve(lv.T, lv.place) * lv.f[0], lv.n, lv.RS, lv.RSl)
+
     def setup_between():
         at = 4 * 64 + 4 * 8
         TP[...] = dot(c1_ref[at : at + 128, :], middle.hot).reshape(16, 8, 128)
         TPT[...] = dot(c1_ref[at + 128 : at + 256, :], middle.hot).reshape(8, 16, 128)
-        PT1[...] = dot(c1_ref[at + 256 : at + 272, :], middle.hot).reshape(2, 8, 128)
+        spread(KEEP, resolve(TP, middle.place), 16, RP, RPl)
+
+    def setup_coarse():
+        at = 4 * 64 + 4 * 8 + 256
+        PT1[...] = dot(c1_ref[at : at + 16, :], middle.hot).reshape(2, 8, 128)
         place1 = middle.place
-        spread(KEEP, resolve(TP, place1), 16, RP, RPl)
         wide = jnp.concatenate([TPT[...], TPT[...]], axis=2)
         spread(KEEP, resolve(wide, fine.place), 8, RPT, RPTl)
         spread(KEEP, jnp.where(place1 == 0, PT1[0], jnp.where(place1 == 1, PT1[1], 0.0)), 8, RP1, RP1l)
@@ -331,9 +337,11 @@
         RPT1l[...] = jnp.zeros(RPT1l.shape, jnp.bfloat16)
         spread(KEEP, resolve(PT1, place1), 2, RPT1, RPT1l)
 
-    def setup_middle():
+    def after_second_send():
+        for load in loads[8:]:
+            load.wait()
         setup_first(middle, 1)
-        setup_rest(middle, 1)
+        setup_return(middle, 1)
         setup_between()
 
     one = lambda cond: jnp.where(cond, 1.0, 0.0).astype(jnp.bfloat16)
@@ -435,34 +443,43 @@
 
     def apply_level(lv, slot_of, number, consume, meanwhile=None, near=None, defer=False, lead=False):
         n, lanes = lv.n, lv.lanes
-        flat = lv.V[...].reshape(n * n, lanes)
-        high, low = split(flat)
+        high, low = split(lv.V[...].reshape(n * n, lanes))
         lv.U[...] = (dot(high, lv.PP[...]) + dot(low, lv.PP[...])).reshape(n, n, 2 * lanes)
-        y0, z0 = lv.V[0], lv.V[:, 0, :]
-        y1, z1 = jnp.zeros_like(y0), jnp.zeros_like(z0)
+        z0 = lv.V[:, 0, :]
+        z1 = jnp.zeros_like(z0)
         for p in lv.last_range:
-            here = lv.last == p
-            y1 = jnp.where(here, lv.V[p], y1)
-            z1 = jnp.where(here, lv.V[:, p, :], z1)
-        turned = dot3(jnp.concatenate([z0, z1, y0, y1], axis=0), lv.RI, lv.RIl)
-        lv.H[2:6] = turned.reshape(4, n, lanes)
+            z1 = jnp.where(lv.last == p, lv.V[:, p, :], z1)
+        turned = dot3(jnp.concatenate([z0, z1], axis=0), lv.RI, lv.RIl)
         for f in range(2):
             total = None
             for j in range(n):
                 term = lv.IL[j : j + 1, :] * lv.U[j, :, f * lanes : (f + 1) * lanes]
                 total = term if total is None else total + term
             lv.H[f] = total
-        lv.Q[...] = contract(lv.TI, lv.H, 0, 6)
+        lv.Q[0:2] = contract(lv.TI, lv.H, 0, 2)
         copies = []
+        start = lambda d, value: copies.append(
+            send(number, d, value, lv.SB.at[slot_of, d], lv.RB.at[slot_of, d])
+        )
         if near is None:
-            outgoing = [lv.Q[0], lv.Q[1], lv.Q[2], towards_first(lv.Q[3], lv.at_last)]
-            copies = [
-                send(number, d, outgoing[d], lv.SB.at[slot_of, d], lv.RB.at[slot_of, d]) for d in range(4)
-            ]
+            start(0, lv.Q[0])
+            start(1, lv.Q[1])
+        lv.H[2:4] = turned.reshape(2, n, lanes)
+        lv.Q[2:4] = contract(lv.TI, lv.H, 2, 2)
+        if near is None:
+            start(2, lv.Q[2])
+            start(3, towards_first(lv.Q[3], lv.at_last))
         if lead:
             return copies
         if meanwhile is not None:
             meanwhile()
+        y0 = lv.V[0]
+        y1 = jnp.zeros_like(y0)
+        for p in lv.last_range:
+            y1 = jnp.where(lv.last == p, lv.V[p], y1)
+        turned = dot3(jnp.concatenate([y0, y1], axis=0), lv.RI, lv.RIl)
+        lv.H[4:6] = turned.reshape(2, n, lanes)
+        lv.Q[4:6] = contract(lv.TI, lv.H, 4, 2)
         lv.G[4] = lv.pair[...] * (lv.Q[4] - jnp.where(lv.row > 0, roll(lv.Q[5], 1), 0.0))
         lv.G[5] = lv.pair[...] * (lv.Q[5] - jnp.where(lv.row < 3, roll(lv.Q[4], -1), 0.0))
         back = contract(lv.TIT, lv.G, 4, 2).reshape(2 * n, lanes)
@@ -544,14 +561,17 @@
         return consume
 
     def after_first_send():
-        for load in loads[8:]:
-            load.wait()
+        setup_return(fine, 0)
+        setup_volume(fine, 0)
+
+    def after_third_send():
         factor_copies.update(gather_start(0, own_factors, REACH - 1))
-        setup_rest(fine, 0)
+        setup_volume(middle, 1)
+        setup_coarse()
 
     first_step(fine)
     apply_level(fine, 0, 0, end_pre(fine), after_first_send)
-    apply_level(fine, 1, 1, remainder(fine), setup_middle, defer=True)
+    apply_level(fine, 1, 1, remainder(fine), after_second_send, defer=True)
 
     lanes_down = dot3(fine.OUT[...].reshape(256, 256), RP, RPl).reshape(16, 16, 128)
     total = None
@@ -577,7 +597,7 @@
     for j in range(8):
         middle.R[j] = middle.R[j] + x_back[j] + z_back(j)
     first_step(middle)
-    apply_level(middle, 0, 2, end_pre(middle))
+    apply_level(middle, 0, 2, end_pre(middle), after_third_send)
     apply_level(middle, 1, 3, remainder(middle), defer=True)
 
     parts = []

time: 62.8 us -> 62.6 us (level)
  no operation moved by 1% of the time
where the time goes in v5:
time: 62.6 us; the launch traced here: 62 us
  Pallas kernels  60.4 us (96%)
  local copies, waits for them, and re-layouts  1.62 us (3%)
    pallas_call x1, Pallas kernels, shards(): pl.pallas_call(functools.partial(kernel, taus, coarse), out_shape=jax.Sha...  60.4 us
    unnamed x1, local copies, waits for them, and re-layouts  1.62 us

profile of v5, /device:TPU:24, one launch (start us, length us, event | category | flops | bytes accessed | tf_op | source)
XLA Modules:
  0.0 62.0 jit_solution(17578383206552692476)
XLA Ops:
  0.0 60.4 %shard_map.154 = f32[1,3,4,4096]{3,2,1,0:T(4,128)} custom-call(s32[4]{0:T(128)} %refs_0_.1, s32[3,1,4]{2,1,0:T(1,128)} %bitcast.7, f32[1,3,4,4]{3,2,1,0:T(4,128)} %bitcast.6, bf16[1088,32]{1,0:T(8,128)(2,1)} %constant.24.clone.refs_3_, bf16[560,32]{1,0:T(8,128)(2,1)} %constant.25.clone.refs_4_, f32[16,256]{1,0:T(8,128)} %constant.26.clone.refs_5_, ...), custom_call_target="tpu_custom_call" | custom-call | tf_op jit(solution)/shard_map/pallas_call | solution.py:835
  60.4 1.6 %copy.18 = f32[1,4,3,4096]{3,1,2,0:T(4,128)} copy(f32[1,4,3,4096]{3,1,2,0:T(4,128)} %bitcast.4) | data formatting | bytes 393216

commit v6 on v4

--- a/solution.py
+++ b/solution.py
@@ -307,23 +307,29 @@
             if index == 0:
                 lv.X[j] = node_live
 
-    def setup_rest(lv, index):
+    def setup_return(lv, index):
         n, lanes = lv.n, lv.lanes
-        for which in (1, 2, 3):
-            tables(lv, index, which)
-        spread(KEEP, resolve(lv.T, lv.place) * lv.f[0], n, lv.RS, lv.RSl)
+        tables(lv, index, 1)
         spread(KEEP, resolve(lv.TIT, lv.place), n, lv.RIT, lv.RITl)
         for p in range(n):
             lv.PPT[p * SLOTS : (p + 1) * SLOTS, :] = one(lv.same & (lv.place == 0))
             lv.PPT[lanes + p * SLOTS : lanes + (p + 1) * SLOTS, :] = one(lv.same & (lv.place == lv.last))
 
+    def setup_volume(lv, index):
+        tables(lv, index, 2)
+        tables(lv, index, 3)
+        spread(KEEP, resolve(lv.T, lv.place) * lv.f[0], lv.n, lv.RS, lv.RSl)
+
     def setup_between():
         at = 4 * 64 + 4 * 8
         TP[...] = dot(c1_ref[at : at + 128, :], middle.hot).reshape(16, 8, 128)
         TPT[...] = dot(c1_ref[at + 128 : at + 256, :], middle.hot).reshape(8, 16, 128)
-        PT1[...] = dot(c1_ref[at + 256 : at + 272, :], middle.hot).reshape(2, 8, 128)
+        spread(KEEP, resolve(TP, middle.place), 16, RP, RPl)
+
+    def setup_coarse():
+        at = 4 * 64 + 4 * 8 + 256
+        PT1[...] = dot(c1_ref[at : at + 16, :], middle.hot).reshape(2, 8, 128)
         place1 = middle.place
-        spread(KEEP, resolve(TP, place1), 16, RP, RPl)
         wide = jnp.concatenate([TPT[...], TPT[...]], axis=2)
         spread(KEEP, resolve(wide, fine.place), 8, RPT, RPTl)
         spread(KEEP, jnp.where(place1 == 0, PT1[0], jnp.where(place1 == 1, PT1[1], 0.0)), 8, RP1, RP1l)
@@ -331,9 +337,11 @@
         RPT1l[...] = jnp.zeros(RPT1l.shape, jnp.bfloat16)
         spread(KEEP, resolve(PT1, place1), 2, RPT1, RPT1l)
 
-    def setup_middle():
+    def after_second_send():
+        for load in loads[8:]:
+            load.wait()
         setup_first(middle, 1)
-        setup_rest(middle, 1)
+        setup_return(middle, 1)
         setup_between()
 
     one = lambda cond: jnp.where(cond, 1.0, 0.0).astype(jnp.bfloat16)
@@ -544,14 +552,17 @@
         return consume
 
     def after_first_send():
-        for load in loads[8:]:
-            load.wait()
+        setup_return(fine, 0)
+        setup_volume(fine, 0)
+
+    def after_third_send():
         factor_copies.update(gather_start(0, own_factors, REACH - 1))
-        setup_rest(fine, 0)
+        setup_volume(middle, 1)
+        setup_coarse()
 
     first_step(fine)
     apply_level(fine, 0, 0, end_pre(fine), after_first_send)
-    apply_level(fine, 1, 1, remainder(fine), setup_middle, defer=True)
+    apply_level(fine, 1, 1, remainder(fine), after_second_send, defer=True)
 
     lanes_down = dot3(fine.OUT[...].reshape(256, 256), RP, RPl).reshape(16, 16, 128)
     total = None
@@ -577,7 +588,7 @@
     for j in range(8):
         middle.R[j] = middle.R[j] + x_back[j] + z_back(j)
     first_step(middle)
-    apply_level(middle, 0, 2, end_pre(middle))
+    apply_level(middle, 0, 2, end_pre(middle), after_third_send)
     apply_level(middle, 1, 3, remainder(middle), defer=True)
 
     parts = []

time: 62.8 us -> 62.5 us (level)
  no operation moved by 1% of the time
where the time goes in v6:
time: 62.5 us; the launch traced here: 61.9 us
  Pallas kernels  60.3 us (96%)
  local copies, waits for them, and re-layouts  1.62 us (3%)
    pallas_call x1, Pallas kernels, shards(): pl.pallas_call(functools.partial(kernel, taus, coarse), out_shape=jax.Sha...  60.3 us
    unnamed x1, local copies, waits for them, and re-layouts  1.62 us

profile of v6, /device:TPU:24, one launch (start us, length us, event | category | flops | bytes accessed | tf_op | source)
XLA Modules:
  0.0 61.9 jit_solution(13120942344148229464)
XLA Ops:
  0.0 60.3 %shard_map.154 = f32[1,3,4,4096]{3,2,1,0:T(4,128)} custom-call(s32[4]{0:T(128)} %refs_0_.1, s32[3,1,4]{2,1,0:T(1,128)} %bitcast.7, f32[1,3,4,4]{3,2,1,0:T(4,128)} %bitcast.6, bf16[1088,32]{1,0:T(8,128)(2,1)} %constant.24.clone.refs_3_, bf16[560,32]{1,0:T(8,128)(2,1)} %constant.25.clone.refs_4_, f32[16,256]{1,0:T(8,128)} %constant.26.clone.refs_5_, ...), custom_call_target="tpu_custom_call" | custom-call | tf_op jit(solution)/shard_map/pallas_call | solution.py:826
  60.3 1.6 %copy.18 = f32[1,4,3,4096]{3,1,2,0:T(4,128)} copy(f32[1,4,3,4096]{3,1,2,0:T(4,128)} %bitcast.4) | data formatting | bytes 393216
